TPU v7x, 256 devices: a whole 4x4x8 slice. The times are simulated.
256 devices in a mesh: expert: 32 (over z, x_lo, core), hidden: 8 (over y, x_hi).
Axes of the slice: x: 4 (x_hi: 2, x_lo: 2; x = x_hi * 2 + x_lo), y: 4, z: 8, core: 2. Of those that a mesh axis runs over, the one named last changes fastest.
Arguments:
- tokens: bfloat16 [768, 7168], P('expert', 'hidden'), may hold values from -6 to 6
- cotangent: bfloat16 [768, 7168], P('expert', 'hidden'), may hold values from -6 to 6
- route_ids: int32 [768, 2], P('expert'), may hold values from 0 to 7, all different within a row; in each aligned block of 24 rows (0 to 23, 24 to 47, ...) at most 10 rows name the same one
- route_gates: float32 [768, 2], P('expert'), may hold values from 0.1 to 0.9
- expert_gate: bfloat16 [8, 4864, 7168], P('hidden', 'expert'), may hold values from -0.0625 to 0.0625
- expert_up: bfloat16 [8, 4864, 7168], P('hidden', 'expert'), may hold values from -0.0625 to 0.0625
- expert_down: bfloat16 [8, 4864, 7168], P('hidden', 'expert'), may hold values from -0.078125 to 0.078125
- dense_gate: bfloat16 [4864, 7168], P('expert', 'hidden'), may hold values from -0.0625 to 0.0625
- dense_up: bfloat16 [4864, 7168], P('expert', 'hidden'), may hold values from -0.0625 to 0.0625
- dense_down: bfloat16 [4864, 7168], P('expert', 'hidden'), may hold values from -0.078125 to 0.078125
Outputs:
- input_grad: bfloat16 [768, 7168], P('expert', 'hidden')
Inputs may be any that keep to these rules, and one draw needn't show every extreme that they name: `route_ids`: each row names two different experts. In each aligned block of 24 rows (the tokens of one index of expert) no expert is named by more than 10 rows, a bound that some block reaches.
All inputs are finite; a program needn't handle non-finite values.
Results may differ from a plain program's by a relative error of at most 0.0039.
Values may be sent and summed in bfloat16 or wider, within the bound.
A program may use at most 128 MiB of HBM per device.

v0:
```python
import jax
import jax.numpy as jnp
from jax import lax
from jax.sharding import PartitionSpec as P


def slot_tables(route_ids, gate_values, experts, capacity):
    count_rows = route_ids.shape[0]
    labels = jnp.arange(experts, dtype=jnp.int32)
    matches = (route_ids[:, :, None] == labels[None, None, :]).astype(jnp.float32)
    flat_hits = matches.reshape(count_rows * 2, experts)
    before = jnp.cumsum(flat_hits, axis=0) - flat_hits
    slot_labels = jnp.arange(capacity).astype(jnp.float32)
    placed = flat_hits[:, :, None] * (before[:, :, None] == slot_labels[None, None, :]).astype(
        jnp.float32
    )
    placed = placed.reshape(count_rows, 2, experts, capacity)
    choose = jnp.einsum("tkec->ect", placed)
    weigh = jnp.einsum("tkec,tk->ect", placed, gate_values, precision=lax.Precision.HIGHEST)
    return (choose, weigh)


def local_grads(pre_gate, pre_up, upstream):
    sigma_a = jax.nn.sigmoid(pre_gate)
    grad_gate = (upstream * pre_up * sigma_a * (1.0 + pre_gate * (1.0 - sigma_a))).astype(
        jnp.bfloat16
    )
    grad_up = (upstream * pre_gate * sigma_a).astype(jnp.bfloat16)
    return (grad_gate, grad_up)


def expert_terms(rows, cot_rows, w_gate, w_up, w_down):
    pre_gate = jnp.dot(rows, w_gate.T, preferred_element_type=jnp.float32)
    pre_up = jnp.dot(rows, w_up.T, preferred_element_type=jnp.float32)
    upstream = jnp.dot(cot_rows, w_down.T, preferred_element_type=jnp.float32)
    grad_gate, grad_up = local_grads(pre_gate, pre_up, upstream)
    return jnp.dot(grad_gate, w_gate, preferred_element_type=jnp.float32) + jnp.dot(
        grad_up, w_up, preferred_element_type=jnp.float32
    )


def on_device(
    tokens,
    cotangent,
    route_ids,
    route_gates,
    expert_gate,
    expert_up,
    expert_down,
    dense_gate,
    dense_up,
    dense_down,
):
    experts = lax.axis_size("hidden")
    tok_count = tokens.shape[0]
    capacity = min(tok_count, 5 * tok_count // (3 * experts) * 2)
    own_index = lax.axis_index("hidden")
    all_tokens, all_cot = (
        lax.all_gather(tokens, "expert", axis=0, tiled=True),
        lax.all_gather(cotangent, "expert", axis=0, tiled=True),
    )
    part_gate = jnp.dot(all_tokens, dense_gate.T, preferred_element_type=jnp.float32)
    part_up = jnp.dot(all_tokens, dense_up.T, preferred_element_type=jnp.float32)
    part_down = jnp.dot(all_cot, dense_down.T, preferred_element_type=jnp.float32)
    part_gate, part_up, part_down = lax.psum((part_gate, part_up, part_down), "hidden")
    dense_ggate, dense_gup = local_grads(part_gate, part_up, part_down)
    expert_slice = None
    full_tokens, full_cot = (
        lax.all_gather(tokens, "hidden", axis=1, tiled=True),
        lax.all_gather(cotangent, "hidden", axis=1, tiled=True),
    )
    choose, weigh = slot_tables(route_ids, route_gates, experts, capacity)
    pick = lax.dynamic_index_in_dim(choose, own_index, 0, keepdims=False).astype(jnp.bfloat16)
    rows = jnp.dot(pick, full_tokens, preferred_element_type=jnp.float32).astype(jnp.bfloat16)
    cot_rows = jnp.dot(pick, full_cot, preferred_element_type=jnp.float32).astype(jnp.bfloat16)
    loop_rows, loop_cot = (
        lax.all_gather(rows, "expert", axis=0, tiled=True),
        lax.all_gather(cot_rows, "expert", axis=0, tiled=True),
    )
    back_rows = expert_terms(loop_rows, loop_cot, expert_gate[0], expert_up[0], expert_down[0])
    back_mine = lax.psum_scatter(back_rows, "expert", scatter_dimension=0, tiled=True)
    weigh_mine = lax.dynamic_index_in_dim(weigh, own_index, 0, keepdims=False)
    expert_cols = jnp.dot(weigh_mine.T, back_mine, precision=lax.Precision.HIGHEST)
    expert_slice = lax.psum_scatter(expert_cols, "hidden", scatter_dimension=1, tiled=True)
    result = jnp.dot(dense_ggate, dense_gate, preferred_element_type=jnp.float32)
    result = result + jnp.dot(dense_gup, dense_up, preferred_element_type=jnp.float32)
    combined = lax.psum_scatter(result, "expert", scatter_dimension=0, tiled=True)
    summed = cotangent.astype(jnp.float32) + combined
    summed = summed + expert_slice
    return summed.astype(jnp.bfloat16)


def solution(mesh):
    in_specs = (
        P("expert", "hidden"),
        P("expert", "hidden"),
        P("expert", None),
        P("expert", None),
        P("hidden", "expert", None),
        P("hidden", "expert", None),
        P("hidden", "expert", None),
        P("expert", "hidden"),
        P("expert", "hidden"),
        P("expert", "hidden"),
    )
    out_specs = P("expert", "hidden")
    return jax.shard_map(
        on_device, mesh=mesh, in_specs=in_specs, out_specs=out_specs, check_vma=False
    )
```

profile of v0, /device:TPU:6, one launch (start us, length us, event | category | flops | bytes accessed | tf_op | source)
XLA Modules:
  0.0 851.9 jit_solution(12168506663460104484)
XLA Ops:
  6.5 0.7 all-gather.9.cloned.1.call-update
  7.3 0.7 all-gather.7.cloned.1.call-update
  8.1 0.8 copy.17
  8.8 0.1 eq.48
  9.1 0.2 fusion.49
  9.5 0.8 select_reduce_fusion
  10.3 36.0 %all_gather.20 = bf16[24,7168]{1,0:T(8,128)(2,1)S(1)} all-gather(bf16[24,896]{1,0:T(8,128)(2,1)} %param.11), channel_id=1, replica_groups=mesh['expert'=32,'hidden'=8] {'hidden'}, dimensions={1}, use_global_device_ids=true | all-gather | bytes 387072 | tf_op jit(solution)/shard_map/all_gather | solution.py:70
  46.2 0.9 fusion
  47.2 36.1 %all_gather.22 = bf16[24,7168]{1,0:T(8,128)(2,1)S(1)} all-gather(bf16[24,896]{1,0:T(8,128)(2,1)} %param.10), channel_id=1, replica_groups=mesh['expert'=32,'hidden'=8] {'hidden'}, dimensions={1}, use_global_device_ids=true | all-gather | bytes 387072 | tf_op jit(solution)/shard_map/all_gather | solution.py:69
  83.3 0.9 fusion.1
  84.4 2.9 fusion.52
  87.3 1.4 fusion.51
  88.7 52.5 %all-gather.7.cloned.1.call-done = bf16[768,896]{1,0:T(8,128)(2,1)} async-done(((bf16[24,896]{1,0:T(8,128)(2,1)}), bf16[768,896]{1,0:T(8,128)(2,1)}) %all-gather.7.cloned.1.call-update) | async-done | bytes 1376272 | tf_op jit(solution)/shard_map/all_gather | solution.py:60
  141.2 2.8 fusion.50
  144.1 70.7 %all-gather.11.cloned.1.call-done = bf16[32,10,7168]{2,1,0:T(8,128)(2,1)} async-done(((bf16[1,10,7168]{2,1,0:T(8,128)(2,1)}), bf16[32,10,7168]{2,1,0:T(8,128)(2,1)}) %all-gather.11.cloned.1.call-update) | async-done | bytes 4587536 | tf_op jit(solution)/shard_map/all_gather | solution.py:78
  214.8 8.0 reshape.78
  222.9 4.8 fusion.9
  227.7 59.8 %all-gather.13.cloned.1.call-done = bf16[32,10,7168]{2,1,0:T(8,128)(2,1)} async-done(((bf16[1,10,7168]{2,1,0:T(8,128)(2,1)}), bf16[32,10,7168]{2,1,0:T(8,128)(2,1)}) %all-gather.13.cloned.1.call-update) | async-done | bytes 4587536 | tf_op jit(solution)/shard_map/all_gather | solution.py:77
  287.5 8.1 reshape.80
  295.6 4.8 fusion.4
  300.5 10.6 %fusion.2 = f32[320,7168]{1,0:T(8,128)} fusion(bf16[1,152,7168]{2,1,0:T(8,128)(2,1)} %param.14, f32[320,152]{0,1:T(8,128)S(1)} %fusion.9, bf16[320,7168]{1,0:T(8,128)(2,1)} %reshape.80, bf16[1,152,7168]{2,1,0:T(8,128)(2,1)S(1)} %copy-done, f32[320,152]{0,1:T(8,128)S(1)} %fusion.4), kind=kOutput, calls=%fused_computation.5 | convolution fusion | flops 1395092480 | bytes 18509824 | tf_op jit(solution)/shard_map/dot_general | solution.py:37
  311.0 8.7 %convolution_add_fusion = f32[320,7168]{1,0:T(8,128)} fusion(f32[320,7168]{1,0:T(8,128)} %fusion.2, bf16[1,152,7168]{2,1,0:T(8,128)(2,1)S(1)} %copy-done, f32[320,152]{0,1:T(8,128)S(1)} %fusion.9, f32[320,152]{0,1:T(8,128)S(1)} %fusion.4), kind=kOutput, calls=%fused_computation | convolution fusion | flops 699888640 | bytes 20918272 | tf_op jit(solution)/shard_map/dot_general | solution.py:37
  319.8 68.1 %all-reduce.8.cloned.1.call-done = (f32[768,152]{0,1:T(8,128)}, f32[768,152]{0,1:T(8,128)}, f32[768,152]{0,1:T(8,128)}) async-done(((f32[768,152]{0,1:T(8,128)}, f32[768,152]{0,1:T(8,128)}, f32[768,152]{0,1:T(8,128)}), (f32[768,152]{0,1:T(8,128)}, f32[768,152]{0,1:T(8,128)}, f32[768,152]{0,1:T(8,128)})) %all-reduce.8.cloned.1.call-update) | async-done | bytes 1400848 | tf_op jit(solution)/shard_map/psum | solution.py:65
  387.9 2.0 fusion.27
  389.9 2.2 convolution_add_fusion.1
  392.3 0.5 copy-done.8
  392.8 0.6 dynamic-slice.5
  394.0 249.6 %all-reduce.6.cloned.1.call-done = f32[320,7168]{1,0:T(8,128)} async-done(((f32[320,7168]{1,0:T(8,128)}), f32[320,7168]{1,0:T(8,128)}) %all-reduce.6.cloned.1.call-update) | async-done | bytes 9175056
  643.6 2.6 fusion.25
  646.2 119.4 %reduce-scatter.8.cloned.1.call-done = f32[24,896]{1,0:T(8,128)} async-done(((f32[768,896]{1,0:T(8,128)}), f32[24,896]{1,0:T(8,128)}) %reduce-scatter.8.cloned.1.call-update) | async-done | bytes 86032
  765.6 77.9 %reduce-scatter.6.cloned.1.call-done = f32[24,896]{1,0:T(8,128)} async-done(((f32[24,7168]{1,0:T(8,128)}), f32[24,896]{1,0:T(8,128)}) %reduce-scatter.6.cloned.1.call-update) | async-done | bytes 86032 | tf_op jit(solution)/shard_map/reduce_scatter | solution.py:84
  843.5 1.6 add_convert_fusion
  (40 shorter events, 0.9 us)
Async XLA Ops:
  6.5 293.9 %copy-start = (bf16[1,152,7168]{2,1,0:T(8,128)(2,1)S(1)}, bf16[1,152,7168]{2,1,0:T(8,128)(2,1)}, u32[]{:S(2)}) copy-start(bf16[1,152,7168]{2,1,0:T(8,128)(2,1)} %param.15) | copy-start | bytes 6537220
  6.5 77.8 %copy-start.4 = (bf16[152,896]{1,0:T(8,128)(2,1)S(1)}, bf16[152,896]{1,0:T(8,128)(2,1)}, u32[]{:S(2)}) copy-start(bf16[152,896]{1,0:T(8,128)(2,1)} %param.17) | copy-start | bytes 817156
  6.5 77.8 %all-gather.9.cloned.1.call-start = ((), (), s32[]{:S(2)}) async-start(), calls=%async_computation.3 | async-start | bytes 1419264 | tf_op jit(solution)/shard_map/all_gather | solution.py:59
  7.3 134.0 %all-gather.7.cloned.1.call-start = ((), (), s32[]{:S(2)}) async-start(), calls=%async_computation.2 | async-start | bytes 1419264 | tf_op jit(solution)/shard_map/all_gather | solution.py:60
  8.0 206.8 %all-gather.11.cloned.1.call-start = ((), (), s32[]{:S(2)}) async-start(), calls=%async_computation.5 | async-start | bytes 7569408 | tf_op jit(solution)/shard_map/all_gather | solution.py:78
  10.3 77.0 %copy-start.5 = (bf16[152,896]{1,0:T(8,128)(2,1)S(1)}, bf16[152,896]{1,0:T(8,128)(2,1)}, u32[]{:S(2)}) copy-start(bf16[152,896]{1,0:T(8,128)(2,1)} %param.18) | copy-start | bytes 817156
  47.2 240.3 %all-gather.13.cloned.1.call-start = ((), (), s32[]{:S(2)}) async-start(), calls=%async_computation.6 | async-start | bytes 7569408 | tf_op jit(solution)/shard_map/all_gather | solution.py:77
  84.3 57.0 %copy-start.7 = (bf16[152,896]{1,0:T(8,128)(2,1)S(1)}, bf16[152,896]{1,0:T(8,128)(2,1)}, u32[]{:S(2)}) copy-start(bf16[152,896]{1,0:T(8,128)(2,1)} %param.19) | copy-start | bytes 817156
  84.3 303.6 %all-reduce.8.cloned.1.call-start = ((), (), s32[]{:S(2)}) async-start(), calls=%async_computation.9 | async-start | bytes 2801664 | tf_op jit(solution)/shard_map/psum | solution.py:65
  84.4 2.9 copy-start.1
  144.0 499.5 %all-reduce.6.cloned.1.call-start = ((), (), s32[]{:S(2)}) async-start(), calls=%async_computation.7 | async-start | bytes 18350080
  319.7 445.9 %reduce-scatter.8.cloned.1.call-start = ((), (), s32[]{:S(2)}) async-start(), calls=%async_computation.8 | async-start | bytes 2838528
  387.9 2.1 copy-start.2
  387.9 2.1 copy-start.3
  392.1 0.7 copy-start.8
  392.1 451.4 %copy-start.6 = (bf16[24,896]{1,0:T(8,128)(2,1)S(1)}, bf16[24,896]{1,0:T(8,128)(2,1)}, u32[]{:S(2)}) copy-start(bf16[24,896]{1,0:T(8,128)(2,1)} %param.11) | copy-start | bytes 129028
  392.1 451.4 %reduce-scatter.6.cloned.1.call-start = ((), (), s32[]{:S(2)}) async-start(), calls=%async_computation.4 | async-start | bytes 774144 | tf_op jit(solution)/shard_map/reduce_scatter | solution.py:84
Sparse Core Ops, SparseCore 0:
  9.2 66.3 all-gather.8
  77.5 63.6 all-gather.6
  143.1 71.6 all-gather.10
  216.5 70.9 all-gather.12
  290.2 97.5 all-reduce.7
  390.4 253.1 all-reduce.5
  646.1 119.4 reduce-scatter.7
  769.5 73.9 reduce-scatter.5
where the time goes:
time: 853 us; the launch traced here: 852 us
  waiting for transfers between devices  699 us (82%)
  blocking collectives  72.1 us (8%)
  matrix products  44.7 us (5%)
  local copies, waits for them, and re-layouts  18.4 us (2%)
  between operations  14.3 us (2%)
    unnamed x10, waiting for transfers between devices  370 us
    reduce_scatter x1, waiting for transfers between devices, on_device(): lax.psum_scatter(expert_cols, 'hidden', scatter_dimension=1, tiled=True)  77.9 us
    all_gather x1, waiting for transfers between devices, on_device(): lax.all_gather(cot_rows, 'expert', axis=0, tiled=True)  70.7 us
    psum x1, waiting for transfers between devices, on_device(): lax.psum((part_gate, part_up, part_down), 'hidden')  68.1 us
    all_gather x1, waiting for transfers between devices, on_device(): lax.all_gather(rows, 'expert', axis=0, tiled=True)  59.8 us
    all_gather x1, waiting for transfers between devices, on_device(): lax.all_gather(cotangent, 'expert', axis=0, tiled=True)  52.5 us
    all_gather x1, blocking collectives, on_device(): lax.all_gather(tokens, 'hidden', axis=1, tiled=True)  36.1 us
    all_gather x1, blocking collectives, on_device(): lax.all_gather(cotangent, 'hidden', axis=1, tiled=True)  36 us
  transfers between devices with their start and end apart: 8, of which 7 were waited for; matrix products, arithmetic and copies ran while one was open for 7% of the time, Pallas kernels for 0%

commit v1 on v0

v1 whole, which is shorter than its diff:
```python
import functools

import jax
import jax.numpy as jnp
from jax import lax
from jax.experimental import pallas as pl
from jax.experimental.pallas import tpu as pltpu
from jax.sharding import PartitionSpec as P

MESH = pl.DeviceIdType.MESH
BF, F32 = jnp.bfloat16, jnp.float32
NZ, NH = 8, 8
TOK, PAD = 24, 32
CAP = 10
PIECE = NZ * CAP
NT = (((1,), (1,)), ((), ()))


def grads_of(pre_gate, pre_up, upstream):
    sigma = 1.0 / (1.0 + jnp.exp(-pre_gate))
    grad_gate = upstream * pre_up * sigma * (1.0 + pre_gate * (1.0 - sigma))
    grad_up = upstream * pre_gate * sigma
    return grad_gate.astype(BF), grad_up.astype(BF)


def iota(shape, dim):
    return lax.broadcasted_iota(jnp.int32, shape, dim)


def kernel(
    tok_ref, cot_ref, meta_ref, wg_hbm, wu_hbm, wd_hbm, dg_ref, du_ref, dd_ref, out_ref,
    wg, wu, wd, toks, meta, pick, rows, pre, gg, gu, keep, give, got, chain_out, chain_in, total,
    x_out, x_in, home_out, home_in, dense_w, part_out, part_in, dgrad, res, res_out, res_in,
    w_sem, s1, r1, s3, r3, ring_s, ring_r, x_s, x_r, core_s, core_r, dw_s, dw_r, da_s, da_r, db_s, db_r, dz_s, dz_r,
    ex_s, ex_r, ch_s, ch_r, xx_s, xx_r, hm_s, hm_r,
):
    e, h = lax.axis_index("expert"), lax.axis_index("hidden")
    z, xl, c = e // 4, (e // 2) % 2, e % 2
    feat = tok_ref.shape[1]
    hid = gg.shape[1]

    def at_z(k):
        return lax.rem(z + (k + NZ) % NZ, NZ)

    def dev(zz, xx, cc, hh):
        return (zz * 4 + xx * 2 + cc, hh)

    def ring(k):
        return dev(at_z(k), xl, c, h)

    x_dev, core_dev = dev(z, 1 - xl, c, h), dev(z, xl, 1 - c, h)
    own, oth = c * 2 + xl, c * 2 + 1 - xl

    def remote(src, dst, send, recv, to):
        return pltpu.make_async_remote_copy(
            src_ref=src, dst_ref=dst, send_sem=send, recv_sem=recv, device_id=to, device_id_type=MESH
        )

    sent = []

    def start(*args):
        copy = remote(*args)
        copy.start()
        sent.append(copy)

    def arrived(dst, recv):
        remote(dst, dst, recv, recv, core_dev).wait_recv()

    loads = [
        pltpu.make_async_copy(src.at[0], dst, w_sem.at[i])
        for i, (src, dst) in enumerate(((wg_hbm, wg), (wu_hbm, wu), (wd_hbm, wd)))
    ]
    for load in loads:
        load.start()

    barrier = pltpu.get_barrier_semaphore()

    def greet(to):
        pl.semaphore_signal(barrier, inc=1, device_id=to, device_id_type=MESH)

    for k in range(1, NZ):
        greet(ring(k))
    for k in range(1, NH):
        greet((e, lax.rem(h + k, NH)))
    greet(x_dev)
    greet(core_dev)

    def home_from(k):
        zs = at_z(-k)
        return dev(zs, xl, c, lax.rem(h + zs, NH))

    for k in range(1, NZ):
        greet(home_from(k))

    @pl.when(z != 0)
    def _():
        greet(home_from(0))

    zero = jnp.zeros((PAD - TOK, feat), F32)
    toks[z, 0] = jnp.concatenate([tok_ref[...].astype(F32), zero], 0).astype(BF)
    toks[z, 1] = jnp.concatenate([cot_ref[...].astype(F32), zero], 0).astype(BF)
    lane = iota(meta_ref.shape, 1)
    meta[z] = jnp.where(lane // PAD == z, meta_ref[...], 0.0)
    hpad = dense_w.shape[2]
    zero = jnp.zeros((hpad - hid, feat), F32)
    for k, ref in enumerate((dg_ref, du_ref, dd_ref)):
        dense_w[own, k] = jnp.concatenate([ref[...].astype(F32), zero], 0).astype(BF)

    pl.semaphore_wait(barrier, (NZ - 1) + (NH - 1) + 2 + (NZ - 1) + (z + NZ - 1) // NZ)

    def token_hop(d, step):
        zs = at_z(-d * (step - 1))
        i = (1 - d) // 2
        start(toks.at[zs], toks.at[zs], s1.at[i, step - 1, 0], r1.at[i, step - 1, 0], ring(d))
        start(meta.at[zs], meta.at[zs], s1.at[i, step - 1, 1], r1.at[i, step - 1, 1], ring(d))

    def token_wait(d, step):
        zs = at_z(-d * step)
        i = (1 - d) // 2
        arrived(toks.at[zs], r1.at[i, step - 1, 0])
        arrived(meta.at[zs], r1.at[i, step - 1, 1])

    token_hop(1, 1)
    token_hop(-1, 1)
    start(dense_w.at[own], dense_w.at[own], dw_s.at[0], dw_r.at[0], x_dev)
    start(dense_w.at[own], dense_w.at[own], dw_s.at[1], dw_r.at[1], core_dev)
    for step in range(1, 5):
        token_wait(1, step)
        if step < 4:
            token_hop(1, step + 1)
            token_wait(-1, step)
            if step < 3:
                token_hop(-1, step + 1)

    q = lax.rem(h + z, NH)
    info = meta[0]
    for k in range(1, NZ):
        info = info + meta[k]
    cols = NZ * PAD
    qf = (q + 1).astype(F32)
    match = jnp.where(info[0:1] == qf, 1.0, jnp.where(info[1:2] == qf, 1.0, 0.0))
    a, b = iota((cols, cols), 0), iota((cols, cols), 1)
    before = jnp.where(a // PAD == b // PAD, jnp.where(a < b, 1.0, 0.0), 0.0).astype(BF)
    rank = jnp.dot(jnp.broadcast_to(match, (8, cols)).astype(BF), before, preferred_element_type=F32)[0:1]
    r, t = iota((PIECE, cols), 0), iota((PIECE, cols), 1)
    slot = (r % CAP).astype(F32)
    choose = jnp.where(r // CAP == t // PAD, jnp.where(rank == slot, match, 0.0), 0.0).astype(BF)
    for k in range(2):
        every = toks[:, k].reshape(cols, feat)
        pick[k] = jnp.dot(choose, every, preferred_element_type=F32).astype(BF)

    slice_dev = dev(z, xl, c, q)
    to_plane = remote(pick, rows.at[z, own], s3.at[0], r3.at[0], slice_dev)
    to_self = pltpu.make_async_copy(pick, rows.at[z, own], r3.at[1])

    @pl.when(z != 0)
    def _():
        to_plane.start()
        to_plane.wait()

    @pl.when(z == 0)
    def _():
        to_self.start()
        to_self.wait()

    def zpos(p):
        return at_z(-p) if p <= 4 else at_z(p - 4)

    def core_send(p, kind):
        ref = rows.at[zpos(p), own if kind < 2 else oth, kind % 2]
        start(ref, ref, core_s.at[p, kind], core_r.at[p, kind], core_dev)

    def x_send(p, kind):
        ref = rows.at[zpos(p), own, kind]
        i = p if kind else 8
        start(ref, ref, x_s.at[i], x_r.at[i], x_dev)

    def x_wait(p, kind):
        arrived(rows.at[zpos(p), oth, kind], x_r.at[p if kind else 8])

    def hop_refs(zs):
        return (rows.at[zs, own, 0], rows.at[zs, own, 1], rows.at[zs, oth, 0])

    def hop(d, step, kind):
        ref = hop_refs(at_z(-d * (step - 1)))[kind]
        i = (1 - d) // 2
        start(ref, ref, ring_s.at[i, step - 1, kind], ring_r.at[i, step - 1, kind], ring(d))

    def hop_wait(d, step, kind):
        ref = hop_refs(at_z(-d * step))[kind]
        arrived(ref, ring_r.at[(1 - d) // 2, step - 1, kind])

    x_send(0, 0)
    for kind in range(2):
        hop(1, 1, kind)
        hop(-1, 1, kind)
    x_send(0, 1)
    core_send(0, 0)
    core_send(0, 1)
    x_wait(0, 0)
    hop(1, 1, 2)
    hop(-1, 1, 2)
    core_send(0, 2)

    def forward(step):
        for kind in range(3):
            for d in (1, -1):
                p = step if d == 1 else step + 4
                last = 4 if d == 1 else 3
                if step > last:
                    continue
                hop_wait(d, step, kind)
                if step < last:
                    hop(d, step + 1, kind)
                if kind == 1:
                    x_send(p, 1)
                core_send(p, kind)

    def relay(p):
        x_wait(p, 1)
        core_send(p, 3)

    def multiply(p):
        for kind in range(4):
            rg = (1 - c) * 2 + (xl if kind < 2 else 1 - xl)
            arrived(rows.at[zpos(p), rg, kind % 2], core_r.at[p, kind])

    def accumulate(p, first=False):
        zs = zpos(p)
        col = pl.ds(pl.multiple_of(lax.rem(h - zs + NH, NH) * feat, 128), feat)
        x = rows[zs, :, 0].reshape(4 * PIECE, feat)
        y = rows[zs, :, 1].reshape(4 * PIECE, feat)
        for k, (lhs, w) in enumerate(((x, wg), (x, wu), (y, wd))):
            new = lax.dot_general(lhs, w[:, col], NT, preferred_element_type=F32)
            pre[k] = new if first else pre[k] + new

    arrived(dense_w.at[oth], dw_r.at[0])
    start(dense_w.at[oth], dense_w.at[oth], dw_s.at[2], dw_r.at[2], core_dev)
    arrived(dense_w.at[(1 - c) * 2 + xl], dw_r.at[1])
    arrived(dense_w.at[(1 - c) * 2 + 1 - xl], dw_r.at[2])
    for k in range(3):
        every = toks[:, k // 2].reshape(cols, feat)
        w = dense_w[:, k].reshape(4 * hpad, feat)
        part = lax.dot_general(every, w, NT, preferred_element_type=F32)
        part_out[:, k] = part.astype(BF).reshape(NH, PAD, 4 * hpad)
    for k in range(1, NH):
        hh = lax.rem(h + k, NH)
        start(part_out.at[hh], part_in.at[k], da_s.at[k], da_r.at[k], (e, hh))

    for load in loads:
        load.wait()
    relay(0)
    multiply(0)
    accumulate(0, True)
    forward(1)

    sums = part_out[h].astype(F32)
    for k in range(1, NH):
        arrived(part_in.at[k], da_r.at[k])
        sums = sums + part_in[k].astype(F32)
    dense_gate, dense_up = grads_of(sums[0], sums[1], sums[2])
    dgrad[h, 0] = dense_gate
    dgrad[h, 1] = dense_up
    for k in range(1, NH):
        start(dgrad.at[h], dgrad.at[h], db_s.at[k], db_r.at[k], (e, lax.rem(h + k, NH)))

    for p in (1, 5):
        relay(p)
        multiply(p)
        accumulate(p)
    forward(2)

    for k in range(1, NH):
        arrived(dgrad.at[lax.rem(h + NH - k, NH)], db_r.at[k])
    result = None
    for k in range(2):
        lhs = dgrad[:, k].reshape(cols, 4 * hpad)
        term = jnp.dot(lhs, dense_w[:, k].reshape(4 * hpad, feat), preferred_element_type=F32)
        result = term if result is None else result + term
    result = result.reshape(NZ, PAD, feat)
    res[...] = result
    res_out[...] = result.astype(BF)
    for k in range(1, NZ):
        start(res_out.at[at_z(k)], res_in.at[k], dz_s.at[k], dz_r.at[k], ring(k))

    for p in (2, 6):
        relay(p)
        multiply(p)
        accumulate(p)
    forward(3)
    for p in (3, 7):
        relay(p)
        multiply(p)
        accumulate(p)
    forward(4)
    relay(4)
    multiply(4)
    accumulate(4)

    new_gate, new_up = grads_of(pre[0], pre[1], pre[2])
    gg[...] = new_gate
    gu[...] = new_up

    def slot_z(i):
        odd = i % 2
        return lax.rem(z + odd * (4 - (i + 1) // 2) + (1 - odd) * (4 + i // 2), NZ)

    half = 2 * PIECE

    def produce(i):
        zd = slot_z(i)
        col = pl.ds(pl.multiple_of(lax.rem(h - zd + NH, NH) * feat, 128), feat)

        def rows_of(cc):
            sel = pl.ds(pl.multiple_of(cc * half, half), half)
            return jnp.dot(gg[sel], wg[:, col], preferred_element_type=F32) + jnp.dot(
                gu[sel], wu[:, col], preferred_element_type=F32
            )

        give[i] = rows_of(1 - c).astype(BF).reshape(2, PIECE, feat)
        start(give.at[i], got.at[i], ex_s.at[i], ex_r.at[i], core_dev)
        keep[i] = rows_of(c).reshape(2, PIECE, feat)

    def mine(i, x):
        return keep[i, x] + got[i, x].astype(F32)

    def chain(d, step, x, i):
        k = (1 - d) // 2
        value = mine(i, x)
        if step == 1 and x == k or step > 1:
            arrived(chain_in.at[k, step - 1, x], ch_r.at[k, step - 1, x])
            value = value + chain_in[k, step - 1, x].astype(F32)
        chain_out[k, step, x] = value.astype(BF)
        start(chain_out.at[k, step, x], chain_in.at[k, step, x], ch_s.at[k, step, x], ch_r.at[k, step, x], ring(d))

    def exchanged(i):
        arrived(got.at[i], ex_r.at[i])

    produce(0)
    produce(1)
    exchanged(0)
    chain(1, 0, 0, 0)
    chain(-1, 0, 1, 0)
    produce(2)
    for step in range(1, 4):
        i = 2 * step - 1
        exchanged(i)
        if step == 1:
            chain(1, 1, 1, i)
        produce(i + 2)
        exchanged(i + 1)
        if step == 1:
            chain(-1, 1, 0, i + 1)
            chain(1, 1, 0, i)
            chain(-1, 1, 1, i + 1)
        else:
            for x in (1, 0):
                chain(1, step, x, i)
                chain(-1, step, 1 - x, i + 1)
        if i + 3 < 8:
            produce(i + 3)
    exchanged(7)
    for x in range(2):
        value = mine(7, x)
        for k in range(2):
            arrived(chain_in.at[k, 3, x], ch_r.at[k, 3, x])
            value = value + chain_in[k, 3, x].astype(F32)
        total[x] = value
    x_out[...] = total[1 - xl].astype(BF)
    start(x_out, x_in, xx_s.at[0], xx_r.at[0], x_dev)
    r, t = iota((NZ * 16, PIECE), 0), iota((NZ * 16, PIECE), 1)
    spread = jnp.where(r % 16 < CAP, jnp.where(t == (r // 16) * CAP + r % 16, 1.0, 0.0), 0.0).astype(BF)
    arrived(x_in, xx_r.at[0])
    final = (total[xl] + x_in[...].astype(F32)).astype(BF)
    home_out[...] = jnp.dot(spread, final, preferred_element_type=F32).astype(BF).reshape(NZ, 16, feat)

    back = lax.rem(h - z + NH, NH)
    for k in range(1, NZ):
        zt = at_z(k)
        start(home_out.at[zt], home_in.at[k], hm_s.at[k], hm_r.at[k], dev(zt, xl, c, back))
    home = remote(home_out.at[z], home_in.at[0], hm_s.at[0], hm_r.at[0], dev(z, xl, c, back))
    stay = pltpu.make_async_copy(home_out.at[z], home_in.at[0], hm_r.at[8])

    @pl.when(z != 0)
    def _():
        home.start()

    @pl.when(z == 0)
    def _():
        stay.start()

    n = NZ * 16
    ids0, ids1 = meta_ref[0:1, 0:n], meta_ref[1:2, 0:n]
    g0, g1 = meta_ref[2:3, 0:n], meta_ref[3:4, 0:n]
    r, t = iota((n, n), 0), iota((n, n), 1)
    label = ((h + (z - r // 16 + NZ) % NZ) % NH + 1).astype(F32)
    hit0, hit1 = jnp.where(ids0 == label, 1.0, 0.0), jnp.where(ids1 == label, 1.0, 0.0)
    before = jnp.where(r // PAD == t // PAD, jnp.where(r < t, 1.0, 0.0), 0.0).astype(BF)
    rank = jnp.dot((hit0 + hit1).astype(BF), before, preferred_element_type=F32)
    weigh = jnp.where(rank == (r % 16).astype(F32), hit0 * g0 + hit1 * g1, 0.0)

    dense = res[z]
    for k in range(1, NZ):
        arrived(res_in.at[k], dz_r.at[k])
        dense = dense + res_in[k].astype(F32)

    for k in range(1, NZ):
        arrived(home_in.at[k], hm_r.at[k])

    @pl.when(z != 0)
    def _():
        home.wait()

    @pl.when(z == 0)
    def _():
        stay.wait()

    expert = lax.dot_general(
        weigh, home_in[...].reshape(n, feat).astype(F32), (((0,), (0,)), ((), ())),
        precision=lax.Precision.HIGHEST, preferred_element_type=F32,
    )
    out_ref[...] = (cot_ref[...].astype(F32) + dense[0:TOK] + expert[0:TOK]).astype(BF)

    for copy in sent:
        copy.wait_send()


def on_device(tokens, cotangent, route_ids, route_gates, expert_gate, expert_up, expert_down, dense_gate, dense_up, dense_down):
    feat = tokens.shape[1]
    hid, width = expert_gate.shape[1], expert_gate.shape[2]
    hpad = (hid + 15) // 16 * 16
    meta = jnp.concatenate([route_ids.astype(F32) + 1.0, route_gates], axis=1).T
    meta = jnp.tile(jnp.pad(meta, ((0, 4), (0, PAD - TOK))), (1, NZ))
    dma, vmem = pltpu.SemaphoreType.DMA, pltpu.VMEM
    scratch = [
        vmem((hid, width), BF), vmem((hid, width), BF), vmem((hid, width), BF),
        vmem((NZ, 2, PAD, feat), BF),
        vmem((NZ, 8, NZ * PAD), F32),
        vmem((2, PIECE, feat), BF),
        vmem((NZ, 4, 2, PIECE, feat), BF),
        vmem((3, 4 * PIECE, hid), F32),
        vmem((4 * PIECE, hid), BF), vmem((4 * PIECE, hid), BF),
        vmem((NZ, 2, PIECE, feat), F32),
        vmem((NZ, 2, PIECE, feat), BF), vmem((NZ, 2, PIECE, feat), BF),
        vmem((2, 4, 2, PIECE, feat), BF), vmem((2, 4, 2, PIECE, feat), BF),
        vmem((2, PIECE, feat), F32),
        vmem((PIECE, feat), BF), vmem((PIECE, feat), BF),
        vmem((NZ, 16, feat), BF), vmem((NZ, 16, feat), BF),
        vmem((4, 3, hpad, feat), BF),
        vmem((NH, 3, PAD, 4 * hpad), BF), vmem((NH, 3, PAD, 4 * hpad), BF),
        vmem((NH, 2, PAD, 4 * hpad), BF),
        vmem((NZ, PAD, feat), F32), vmem((NZ, PAD, feat), BF), vmem((NZ, PAD, feat), BF),
        dma((3,)), dma((2, 4, 2)), dma((2, 4, 2)), dma((2,)), dma((2,)),
        dma((2, 4, 3)), dma((2, 4, 3)), dma((9,)), dma((9,)), dma((8, 4)), dma((8, 4)),
        dma((3,)), dma((3,)), dma((8,)), dma((8,)), dma((8,)), dma((8,)), dma((8,)), dma((8,)),
        dma((8,)), dma((8,)), dma((2, 4, 2)), dma((2, 4, 2)), dma((1,)), dma((1,)), dma((9,)), dma((9,)),
    ]
    whole, far = pl.BlockSpec(memory_space=pltpu.VMEM), pl.BlockSpec(memory_space=pl.ANY)
    return pl.pallas_call(
        kernel,
        out_shape=jax.ShapeDtypeStruct(tokens.shape, BF),
        in_specs=[whole] * 3 + [far] * 3 + [whole] * 3,
        out_specs=whole,
        scratch_shapes=scratch,
        compiler_params=pltpu.CompilerParams(collective_id=0, has_side_effects=True, vmem_limit_bytes=56 << 20),
        name="layer",
    )(tokens, cotangent, meta, expert_gate, expert_up, expert_down, dense_gate, dense_up, dense_down)


def solution(mesh):
    in_specs = (
        P("expert", "hidden"),
        P("expert", "hidden"),
        P("expert", None),
        P("expert", None),
        P("hidden", "expert", None),
        P("hidden", "expert", None),
        P("hidden", "expert", None),
        P("expert", "hidden"),
        P("expert", "hidden"),
        P("expert", "hidden"),
    )
    return jax.shard_map(on_device, mesh=mesh, in_specs=in_specs, out_specs=P("expert", "hidden"), check_vma=False)
```

time: 853 us -> 152 us (0.18)
  waiting for transfers between devices: 699 us -> 0 us
  Pallas kernels: 0 us -> 146 us
  blocking collectives: 72.1 us -> 0 us
  matrix products: 44.7 us -> 0 us
  local copies, waits for them, and re-layouts: 18.4 us -> 2.09 us
  between operations: 14.3 us -> 0.01 us
    unnamed x10 -> x0, waiting for transfers between devices: 370 us -> none
    all_gather x4 -> x0, waiting for transfers between devices: 183 us -> none  [the longest x1 70.7 us: on_device(): lax.all_gather(cot_rows, 'expert', axis=0, tiled=True)]
    pallas_call x0 -> x1, Pallas kernels: none -> 146 us  [on_device(): pl.pallas_call(kernel, out_shape=jax.ShapeDtypeStruct(tokens.shape, BF),...]
    reduce_scatter x1 -> x0, waiting for transfers between devices: 77.9 us -> none  [on_device(): lax.psum_scatter(expert_cols, 'hidden', scatter_dimension=1, tiled=True)]
    all_gather x2 -> x0, blocking collectives: 72.1 us -> none  [the longest x1 36.1 us: on_device(): lax.all_gather(tokens, 'hidden', axis=1, tiled=True)]
    psum x1 -> x0, waiting for transfers between devices: 68.1 us -> none  [on_device(): lax.psum((part_gate, part_up, part_down), 'hidden')]
    dot_general x12 -> x0, matrix products: 44.7 us -> none  [the longest x1 10.6 us: expert_terms(): jnp.dot(grad_gate, w_gate, preferred_element_type=jnp.float32)]
    unnamed x23 -> x1, local copies, waits for them, and re-layouts: 18.1 us -> 1.41 us
  transfers between devices with their start and end apart: 8 -> 0, of which waited for: 7 -> 0; matrix products, arithmetic and copies ran while one was open for 7% -> 0% of each run, Pallas kernels for 0% -> 0%
where the time goes in v1:
time: 152 us; the launch traced here: 150 us
  Pallas kernels  146 us (96%)
  local copies, waits for them, and re-layouts  2.09 us (1%)
    pallas_call x1, Pallas kernels, on_device(): pl.pallas_call(kernel, out_shape=jax.ShapeDtypeStruct(tokens.shape, BF),...  146 us

profile of v1, /device:TPU:6, one launch (start us, length us, event | category | flops | bytes accessed | tf_op | source)
XLA Modules:
  0.0 149.9 jit_solution(6169050209251539282)
XLA Ops:
  0.0 0.7 convert_add_fusion
  0.7 0.7 maximum_bitcast_fusion
  1.4 0.7 tile.10.meta_ref
  2.1 146.4 %layer.1 = bf16[24,896]{1,0:T(8,128)(2,1)} custom-call(bf16[24,896]{1,0:T(8,128)(2,1)} %tok_ref.1, bf16[24,896]{1,0:T(8,128)(2,1)} %cot_ref.1, f32[8,256]{1,0:T(8,128)} %tile.10.meta_ref, bf16[1,152,7168]{2,1,0:T(8,128)(2,1)} %wg_hbm.1, bf16[1,152,7168]{2,1,0:T(8,128)(2,1)} %wu_hbm.1, bf16[1,152,7168]{2,1,0:T(8,128)(2,1)} %wd_hbm.1, ...), custom_call_target="tpu_custom_call" | custom-call | tf_op jit(solution)/shard_map/layer/pallas_call | solution.py:459
  148.5 1.4 copy.12
  (2 shorter events, 0.0 us)

commit v2 on v1

v2 whole, which is shorter than its diff:
```python
import functools

import jax
import jax.numpy as jnp
from jax import lax
from jax.experimental import pallas as pl
from jax.experimental.pallas import tpu as pltpu
from jax.sharding import PartitionSpec as P

MESH = pl.DeviceIdType.MESH
BF, F32 = jnp.bfloat16, jnp.float32
NZ, NH = 8, 8
TOK, PAD = 24, 32
BLOCK = 2 * TOK
CAP = 10
PIECE = NZ * CAP
NT = (((1,), (1,)), ((), ()))


def grads_of(pre_gate, pre_up, upstream):
    sigma = 1.0 / (1.0 + jnp.exp(-pre_gate))
    grad_gate = upstream * pre_up * sigma * (1.0 + pre_gate * (1.0 - sigma))
    grad_up = upstream * pre_gate * sigma
    return grad_gate.astype(BF), grad_up.astype(BF)


def iota(shape, dim):
    return lax.broadcasted_iota(jnp.int32, shape, dim)


def kernel(
    tok_ref, cot_ref, meta_ref, wg_hbm, wu_hbm, wd_hbm, dg_ref, du_ref, dd_ref, out_ref,
    wg, wu, wd, toks, meta, pick, rows, pre, gg, gu, keep, give, got, chain_out, chain_in, total,
    x_out, x_in, home_out, home_in, dense_w, part_out, part_in, dgrad, res, res_x_out, res_x_in, res_out, res_in,
    w_sem, s1, r1, s3, r3, ring_s, ring_r, x_s, x_r, core_s, core_r, dw_s, dw_r, da_s, da_r, db_s, db_r, dz_s, dz_r,
    ex_s, ex_r, ch_s, ch_r, xx_s, xx_r, hm_s, hm_r,
):
    e, h = lax.axis_index("expert"), lax.axis_index("hidden")
    z, xl, c = e // 4, (e // 2) % 2, e % 2
    feat = tok_ref.shape[1]
    hid = gg.shape[1]

    def at_z(k):
        return lax.rem(z + (k + NZ) % NZ, NZ)

    def dev(zz, xx, cc, hh):
        return (zz * 4 + xx * 2 + cc, hh)

    def ring(k):
        return dev(at_z(k), xl, c, h)

    x_dev, core_dev = dev(z, 1 - xl, c, h), dev(z, xl, 1 - c, h)

    def remote(src, dst, send, recv, to):
        return pltpu.make_async_remote_copy(
            src_ref=src, dst_ref=dst, send_sem=send, recv_sem=recv, device_id=to, device_id_type=MESH
        )

    sent = []

    def start(*args):
        copy = remote(*args)
        copy.start()
        sent.append(copy)

    def arrived(dst, recv):
        remote(dst, dst, recv, recv, core_dev).wait_recv()

    loads = [
        pltpu.make_async_copy(src.at[0], dst, w_sem.at[i])
        for i, (src, dst) in enumerate(((wg_hbm, wg), (wu_hbm, wu), (wd_hbm, wd)))
    ]
    for load in loads:
        load.start()

    barrier = pltpu.get_barrier_semaphore()

    def greet(to):
        pl.semaphore_signal(barrier, inc=1, device_id=to, device_id_type=MESH)

    for k in range(1, NZ):
        greet(ring(k))
    for k in range(1, NH):
        greet((e, lax.rem(h + k, NH)))
    greet(x_dev)
    greet(core_dev)

    def home_from(k):
        zs = at_z(-k)
        return dev(zs, xl, c, lax.rem(h + zs, NH))

    for k in range(1, NZ):
        greet(home_from(k))

    @pl.when(z != 0)
    def _():
        greet(home_from(0))

    toks[xl, z] = jnp.concatenate([tok_ref[...].astype(F32), cot_ref[...].astype(F32)], 0).astype(BF)
    lane = iota(meta_ref.shape, 1)
    meta[xl, z] = jnp.where(lane // BLOCK == z, meta_ref[...], 0.0)
    hpad = dense_w.shape[2]
    zero = jnp.zeros((hpad - hid, feat), F32)
    for k, ref in enumerate((dg_ref, du_ref, dd_ref)):
        dense_w[k, c] = jnp.concatenate([ref[...].astype(F32), zero], 0).astype(BF)

    pl.semaphore_wait(barrier, (NZ - 1) + (NH - 1) + 2 + (NZ - 1) + (z + NZ - 1) // NZ)

    def zpos(p):
        return at_z(-p) if p <= 4 else at_z(p - 4)

    def token_hop(d, step):
        zs = at_z(-d * (step - 1))
        i = (1 - d) // 2
        start(toks.at[xl, zs], toks.at[xl, zs], s1.at[i, step - 1, 0], r1.at[i, step - 1, 0], ring(d))
        start(meta.at[xl, zs], meta.at[xl, zs], s1.at[i, step - 1, 1], r1.at[i, step - 1, 1], ring(d))

    def token_wait(d, step):
        zs = at_z(-d * step)
        i = (1 - d) // 2
        arrived(toks.at[xl, zs], r1.at[i, step - 1, 0])
        arrived(meta.at[xl, zs], r1.at[i, step - 1, 1])

    def token_x(p):
        zs = zpos(p)
        start(toks.at[xl, zs], toks.at[xl, zs], x_s.at[p, 0], x_r.at[p, 0], x_dev)
        start(meta.at[xl, zs], meta.at[xl, zs], x_s.at[p, 1], x_r.at[p, 1], x_dev)

    token_hop(1, 1)
    token_hop(-1, 1)
    token_x(0)
    for k in range(3):
        start(dense_w.at[k, c], dense_w.at[k, c], dw_s.at[k], dw_r.at[k], core_dev)
    for step in range(1, 5):
        token_wait(1, step)
        if step < 4:
            token_hop(1, step + 1)
        token_x(step)
        if step < 4:
            token_wait(-1, step)
            if step < 3:
                token_hop(-1, step + 1)
            token_x(step + 4)
    for p in range(NZ):
        zs = zpos(p)
        arrived(toks.at[1 - xl, zs], x_r.at[p, 0])
        arrived(meta.at[1 - xl, zs], x_r.at[p, 1])

    y, xh = h // 2, h % 2

    def plane(dy, flip):
        return lax.rem(y + dy + 8, 4) * 2 + (1 - xh if flip else xh)

    targets = (plane(-z, True), plane(2, False), plane(1, False), plane(-1, False), h)
    cols = NZ * BLOCK
    row = iota((8, cols), 0)
    label = jnp.full((8, cols), -1, jnp.int32)
    for i, q in enumerate(targets):
        label = jnp.where(row == i, q + 1, label)
    label = label.astype(F32)
    a, b = iota((cols, cols), 0), iota((cols, cols), 1)
    before = jnp.where(a // TOK == b // TOK, jnp.where(a < b, 1.0, 0.0), 0.0).astype(BF)
    matches, ranks = [], []
    for x in range(2):
        info = meta[x, 0]
        for k in range(1, NZ):
            info = info + meta[x, k]
        match = jnp.where(info[0:1] == label, 1.0, jnp.where(info[1:2] == label, 1.0, 0.0))
        matches.append(match)
        ranks.append(jnp.dot(match.astype(BF), before, preferred_element_type=F32))
    r, t = iota((2 * PIECE, cols), 0), iota((2 * PIECE, cols), 1)
    slot = (r % CAP).astype(F32)
    inside = t // TOK == (r % PIECE) // CAP * 2 + r // PIECE

    def chosen(i, x):
        choose = jnp.where(inside, jnp.where(ranks[x][i : i + 1] == slot, matches[x][i : i + 1], 0.0), 0.0)
        every = toks[x].reshape(cols, feat)
        both = jnp.dot(choose.astype(BF), every, preferred_element_type=F32).astype(BF)
        return both.reshape(2, PIECE, feat)

    for i in range(4):
        for x in range(2):
            both = chosen(i, x)
            for k in range(2):
                pick[i, k, x] = both[k]
        for k in range(4):
            start(
                pick.at[i, k // 2, k % 2], rows.at[h, c, k // 2, k % 2], s3.at[i, k], r3.at[i, k],
                (e, targets[i]),
            )
    for x in range(2):
        both = chosen(4, x)
        for k in range(2):
            rows[h, c, k, x] = both[k]

    slices = (h, plane(-2, False), plane(-1, False), plane(1, False), plane(z, True), plane(z - 1, True), plane(z + 1, True), plane(z + 2, True))

    def chunk(p, k):
        return rows.at[slices[p], c, k // 2, k % 2]

    def core_send(p, k):
        start(chunk(p, k), chunk(p, k), core_s.at[p, k], core_r.at[p, k], core_dev)

    def hop(d, step, k):
        ref = chunk(4 if step == 0 else (5 if d == 1 else 6), k)
        i = (1 - d) // 2
        start(ref, ref, ring_s.at[i, step, k], ring_r.at[i, step, k], ring(d))

    def multiply(p):
        for k in range(4):
            arrived(rows.at[slices[p], 1 - c, k // 2, k % 2], core_r.at[p, k])

    def accumulate(p, first=False):
        multiply(p)
        sl = slices[p]
        col = pl.ds(pl.multiple_of(sl * feat, 128), feat)
        x = rows[sl, :, 0].reshape(4 * PIECE, feat)
        y = rows[sl, :, 1].reshape(4 * PIECE, feat)
        for k, (lhs, w) in enumerate(((x, wg), (x, wu), (y, wd))):
            new = lax.dot_general(lhs, w[:, col], NT, preferred_element_type=F32)
            pre[k] = new if first else pre[k] + new

    for k in range(4):
        core_send(0, k)

    for k in range(3):
        arrived(dense_w.at[k, 1 - c], dw_r.at[k])
    every = toks[...].reshape(2 * cols, feat)
    for k in range(3):
        w = dense_w[k].reshape(2 * hpad, feat)
        part = lax.dot_general(every, w, NT, preferred_element_type=F32).reshape(2, NZ, BLOCK, 2 * hpad)
        part = part[:, :, 0:TOK] if k < 2 else part[:, :, TOK:BLOCK]
        for hh in range(NH):
            part_out[hh, k] = jnp.concatenate([part[0, hh], part[1, hh]], 0).astype(BF)
    for k in range(1, NH):
        hh = lax.rem(h + k, NH)
        start(part_out.at[hh], part_in.at[k], da_s.at[k], da_r.at[k], (e, hh))

    for k in range(4):
        arrived(chunk(4, k), r3.at[0, k])
        hop(1, 0, k)
        hop(-1, 0, k)
        core_send(4, k)

    for load in loads:
        load.wait()
    accumulate(0, True)

    for i in (2, 3):
        for k in range(4):
            arrived(chunk(i, k), r3.at[i, k])
            core_send(i, k)
    for k in range(4):
        for d in (1, -1):
            arrived(chunk(5 if d == 1 else 6, k), ring_r.at[(1 - d) // 2, 0, k])
            if (k < 2) == (d == 1):
                hop(d, 1, k)
            core_send(5 if d == 1 else 6, k)
    accumulate(4)
    accumulate(2)
    accumulate(3)
    for k in range(4):
        arrived(chunk(1, k), r3.at[1, k])
        core_send(1, k)
    for k in range(4):
        arrived(chunk(7, k), ring_r.at[k // 2, 1, k])
        core_send(7, k)
    accumulate(5)
    accumulate(6)
    accumulate(1)

    sums = part_out[h].astype(F32)
    for k in range(1, NH):
        arrived(part_in.at[k], da_r.at[k])
        sums = sums + part_in[k].astype(F32)
    dense_gate, dense_up = grads_of(sums[0], sums[1], sums[2])
    dgrad[0, h] = dense_gate
    dgrad[1, h] = dense_up
    for k in range(1, NH):
        start(dgrad.at[:, h], dgrad.at[:, h], db_s.at[k], db_r.at[k], (e, lax.rem(h + k, NH)))

    accumulate(7)

    def dense_result():
        for k in range(1, NH):
            arrived(dgrad.at[:, lax.rem(h + NH - k, NH)], db_r.at[k])
        result = None
        for k in range(2):
            lhs = dgrad[k].reshape(cols, 2 * hpad)
            term = jnp.dot(lhs, dense_w[k].reshape(2 * hpad, feat), preferred_element_type=F32)
            result = term if result is None else result + term
        result = result.reshape(NZ, 2, TOK, feat)
        for x in range(2):
            res[x] = result[:, x]
        res_x_out[...] = res[1 - xl].reshape(NZ * TOK, feat).astype(BF)
        start(res_x_out, res_x_in, xx_s.at[1], xx_r.at[1], x_dev)

    def dense_reduce():
        arrived(res_x_in, xx_r.at[1])
        result = res[xl] + res_x_in[...].astype(F32).reshape(NZ, TOK, feat)
        res[xl] = result
        zero = jnp.zeros((PAD - TOK, feat), F32)
        for k in range(NZ):
            res_out[k] = jnp.concatenate([result[k], zero], 0).astype(BF)
        for k in range(1, NZ):
            start(res_out.at[at_z(k)], res_in.at[k], dz_s.at[k], dz_r.at[k], ring(k))

    new_gate, new_up = grads_of(pre[0], pre[1], pre[2])
    gg[...] = new_gate
    gu[...] = new_up

    def slot_z(i):
        odd = i % 2
        return lax.rem(z + odd * (4 - (i + 1) // 2) + (1 - odd) * (4 + i // 2), NZ)

    half = 2 * PIECE

    def produce(i):
        zd = slot_z(i)
        col = pl.ds(pl.multiple_of(lax.rem(h - zd + NH, NH) * feat, 128), feat)

        def rows_of(cc):
            sel = pl.ds(pl.multiple_of(cc * half, half), half)
            return jnp.dot(gg[sel], wg[:, col], preferred_element_type=F32) + jnp.dot(
                gu[sel], wu[:, col], preferred_element_type=F32
            )

        give[i] = rows_of(1 - c).astype(BF).reshape(2, PIECE, feat)
        start(give.at[i], got.at[i], ex_s.at[i], ex_r.at[i], core_dev)
        keep[i] = rows_of(c).reshape(2, PIECE, feat)

    def mine(i, x):
        return keep[i, x] + got[i, x].astype(F32)

    def chain(d, step, x, i):
        k = (1 - d) // 2
        value = mine(i, x)
        if step == 1 and x == k or step > 1:
            arrived(chain_in.at[k, step - 1, x], ch_r.at[k, step - 1, x])
            value = value + chain_in[k, step - 1, x].astype(F32)
        chain_out[k, step, x] = value.astype(BF)
        start(chain_out.at[k, step, x], chain_in.at[k, step, x], ch_s.at[k, step, x], ch_r.at[k, step, x], ring(d))

    def exchanged(i):
        arrived(got.at[i], ex_r.at[i])

    produce(0)
    produce(1)
    exchanged(0)
    chain(1, 0, 0, 0)
    chain(-1, 0, 1, 0)
    produce(2)
    for step in range(1, 4):
        i = 2 * step - 1
        exchanged(i)
        if step == 1:
            chain(1, 1, 1, i)
        produce(i + 2)
        exchanged(i + 1)
        if step == 1:
            chain(-1, 1, 0, i + 1)
            chain(1, 1, 0, i)
            chain(-1, 1, 1, i + 1)
        else:
            for x in (1, 0):
                chain(1, step, x, i)
                chain(-1, step, 1 - x, i + 1)
        if i + 3 < 8:
            produce(i + 3)
        if step == 2:
            dense_result()
        if step == 3:
            dense_reduce()
    exchanged(7)
    for x in range(2):
        value = mine(7, x)
        for k in range(2):
            arrived(chain_in.at[k, 3, x], ch_r.at[k, 3, x])
            value = value + chain_in[k, 3, x].astype(F32)
        total[x] = value
    x_out[...] = total[1 - xl].astype(BF)
    start(x_out, x_in, xx_s.at[0], xx_r.at[0], x_dev)
    r, t = iota((NZ * 16, PIECE), 0), iota((NZ * 16, PIECE), 1)
    spread = jnp.where(r % 16 < CAP, jnp.where(t == (r // 16) * CAP + r % 16, 1.0, 0.0), 0.0).astype(BF)
    arrived(x_in, xx_r.at[0])
    final = (total[xl] + x_in[...].astype(F32)).astype(BF)
    home_out[...] = jnp.dot(spread, final, preferred_element_type=F32).astype(BF).reshape(NZ, 16, feat)

    back = lax.rem(h - z + NH, NH)
    for k in range(1, NZ):
        zt = at_z(k)
        start(home_out.at[zt], home_in.at[k], hm_s.at[k], hm_r.at[k], dev(zt, xl, c, back))
    home = remote(home_out.at[z], home_in.at[0], hm_s.at[0], hm_r.at[0], dev(z, xl, c, back))
    stay = pltpu.make_async_copy(home_out.at[z], home_in.at[0], hm_r.at[8])

    @pl.when(z != 0)
    def _():
        home.start()

    @pl.when(z == 0)
    def _():
        stay.start()

    n = NZ * 16
    ids0, ids1 = meta_ref[0:1, 0:n], meta_ref[1:2, 0:n]
    g0, g1 = meta_ref[2:3, 0:n], meta_ref[3:4, 0:n]
    r, t = iota((n, n), 0), iota((n, n), 1)
    label = ((h + (z - r // 16 + NZ) % NZ) % NH + 1).astype(F32)
    hit0, hit1 = jnp.where(ids0 == label, 1.0, 0.0), jnp.where(ids1 == label, 1.0, 0.0)
    before = jnp.where(r // TOK == t // TOK, jnp.where(r < t, 1.0, 0.0), 0.0).astype(BF)
    rank = jnp.dot((hit0 + hit1).astype(BF), before, preferred_element_type=F32)
    weigh = jnp.where(rank == (r % 16).astype(F32), hit0 * g0 + hit1 * g1, 0.0)

    dense = res[xl, z]
    for k in range(1, NZ):
        arrived(res_in.at[k], dz_r.at[k])
        dense = dense + res_in[k, 0:TOK].astype(F32)

    for k in range(1, NZ):
        arrived(home_in.at[k], hm_r.at[k])

    @pl.when(z != 0)
    def _():
        home.wait()

    @pl.when(z == 0)
    def _():
        stay.wait()

    expert = lax.dot_general(
        weigh, home_in[...].reshape(n, feat).astype(F32), (((0,), (0,)), ((), ())),
        precision=lax.Precision.HIGHEST, preferred_element_type=F32,
    )
    out_ref[...] = (cot_ref[...].astype(F32) + dense + expert[0:TOK]).astype(BF)

    for copy in sent:
        copy.wait_send()


def on_device(tokens, cotangent, route_ids, route_gates, expert_gate, expert_up, expert_down, dense_gate, dense_up, dense_down):
    feat = tokens.shape[1]
    hid, width = expert_gate.shape[1], expert_gate.shape[2]
    hpad = (hid + 15) // 16 * 16
    meta = jnp.concatenate([route_ids.astype(F32) + 1.0, route_gates], axis=1).T
    meta = jnp.tile(jnp.pad(meta, ((0, 4), (0, 0))), (1, 2 * NZ))
    dma, vmem = pltpu.SemaphoreType.DMA, pltpu.VMEM
    scratch = [
        vmem((hid, width), BF), vmem((hid, width), BF), vmem((hid, width), BF),
        vmem((2, NZ, BLOCK, feat), BF),
        vmem((2, NZ, 8, NZ * BLOCK), F32),
        vmem((4, 2, 2, PIECE, feat), BF),
        vmem((NH, 2, 2, 2, PIECE, feat), BF),
        vmem((3, 4 * PIECE, hid), F32),
        vmem((4 * PIECE, hid), BF), vmem((4 * PIECE, hid), BF),
        vmem((NZ, 2, PIECE, feat), F32),
        vmem((NZ, 2, PIECE, feat), BF), vmem((NZ, 2, PIECE, feat), BF),
        vmem((2, 4, 2, PIECE, feat), BF), vmem((2, 4, 2, PIECE, feat), BF),
        vmem((2, PIECE, feat), F32),
        vmem((PIECE, feat), BF), vmem((PIECE, feat), BF),
        vmem((NZ, 16, feat), BF), vmem((NZ, 16, feat), BF),
        vmem((3, 2, hpad, feat), BF),
        vmem((NH, 3, BLOCK, 2 * hpad), BF), vmem((NH, 3, BLOCK, 2 * hpad), BF),
        vmem((2, NH, BLOCK, 2 * hpad), BF),
        vmem((2, NZ, TOK, feat), F32),
        vmem((NZ * TOK, feat), BF), vmem((NZ * TOK, feat), BF),
        vmem((NZ, PAD, feat), BF), vmem((NZ, PAD, feat), BF),
        dma((3,)), dma((2, 4, 2)), dma((2, 4, 2)), dma((4, 4)), dma((4, 4)),
        dma((2, 2, 4)), dma((2, 2, 4)), dma((8, 2)), dma((8, 2)), dma((8, 4)), dma((8, 4)),
        dma((3,)), dma((3,)), dma((8,)), dma((8,)), dma((8,)), dma((8,)), dma((8,)), dma((8,)),
        dma((8,)), dma((8,)), dma((2, 4, 2)), dma((2, 4, 2)), dma((2,)), dma((2,)), dma((9,)), dma((9,)),
    ]
    whole, far = pl.BlockSpec(memory_space=pltpu.VMEM), pl.BlockSpec(memory_space=pl.ANY)
    return pl.pallas_call(
        kernel,
        out_shape=jax.ShapeDtypeStruct(tokens.shape, BF),
        in_specs=[whole] * 3 + [far] * 3 + [whole] * 3,
        out_specs=whole,
        scratch_shapes=scratch,
        compiler_params=pltpu.CompilerParams(collective_id=0, has_side_effects=True, vmem_limit_bytes=56 << 20),
        name="layer",
    )(tokens, cotangent, meta, expert_gate, expert_up, expert_down, dense_gate, dense_up, dense_down)


def solution(mesh):
    in_specs = (
        P("expert", "hidden"),
        P("expert", "hidden"),
        P("expert", None),
        P("expert", None),
        P("hidden", "expert", None),
        P("hidden", "expert", None),
        P("hidden", "expert", None),
        P("expert", "hidden"),
        P("expert", "hidden"),
        P("expert", "hidden"),
    )
    return jax.shard_map(on_device, mesh=mesh, in_specs=in_specs, out_specs=P("expert", "hidden"), check_vma=False)
```

time: 152 us -> 140 us (0.921)
  Pallas kernels: 146 us -> 134 us
    pallas_call x1, Pallas kernels: 146 us -> 134 us  [on_device(): pl.pallas_call(kernel, out_shape=jax.ShapeDtypeStruct(tokens.shape, BF),...]
where the time goes in v2:
time: 140 us; the launch traced here: 138 us
  Pallas kernels  134 us (96%)
  local copies, waits for them, and re-layouts  2.11 us (2%)
    pallas_call x1, Pallas kernels, on_device(): pl.pallas_call(kernel, out_shape=jax.ShapeDtypeStruct(tokens.shape, BF),...  134 us

profile of v2, /device:TPU:6, one launch (start us, length us, event | category | flops | bytes accessed | tf_op | source)
XLA Modules:
  0.0 137.6 jit_solution(11145200162179124178)
XLA Ops:
  0.0 0.7 convert_add_fusion
  0.7 0.7 maximum_bitcast_fusion
  1.4 0.7 tile.10.meta_ref
  2.1 134.1 %layer.1 = bf16[24,896]{1,0:T(8,128)(2,1)} custom-call(bf16[24,896]{1,0:T(8,128)(2,1)} %tok_ref.1, bf16[24,896]{1,0:T(8,128)(2,1)} %cot_ref.1, f32[8,384]{1,0:T(8,128)} %tile.10.meta_ref, bf16[1,152,7168]{2,1,0:T(8,128)(2,1)} %wg_hbm.1, bf16[1,152,7168]{2,1,0:T(8,128)(2,1)} %wu_hbm.1, bf16[1,152,7168]{2,1,0:T(8,128)(2,1)} %wd_hbm.1, ...), custom_call_target="tpu_custom_call" | custom-call | tf_op jit(solution)/shard_map/layer/pallas_call | solution.py:473
  136.2 1.4 %copy.12 = bf16[24,896]{1,0:T(8,128)(2,1)} copy(bf16[24,896]{1,0:T(8,128)(2,1)} %layer.1) | data formatting | bytes 86016
  (2 shorter events, 0.0 us)

commit v3 on v2

--- a/solution.py
+++ b/solution.py
@@ -29,7 +29,7 @@
 
 
 def kernel(
-    tok_ref, cot_ref, meta_ref, wg_hbm, wu_hbm, wd_hbm, dg_ref, du_ref, dd_ref, out_ref,
+    tok_ref, cot_ref, ids_ref, gates_ref, wg_hbm, wu_hbm, wd_hbm, dg_ref, du_ref, dd_ref, out_ref,
     wg, wu, wd, toks, meta, pick, rows, pre, gg, gu, keep, give, got, chain_out, chain_in, total,
     x_out, x_in, home_out, home_in, dense_w, part_out, part_in, dgrad, res, res_x_out, res_x_in, res_out, res_in,
     w_sem, s1, r1, s3, r3, ring_s, ring_r, x_s, x_r, core_s, core_r, dw_s, dw_r, da_s, da_r, db_s, db_r, dz_s, dz_r,
@@ -97,8 +97,18 @@
         greet(home_from(0))
 
     toks[xl, z] = jnp.concatenate([tok_ref[...].astype(F32), cot_ref[...].astype(F32)], 0).astype(BF)
-    lane = iota(meta_ref.shape, 1)
-    meta[xl, z] = jnp.where(lane // BLOCK == z, meta_ref[...], 0.0)
+    cols = NZ * BLOCK
+    t, lane = iota((TOK, cols), 0), iota((TOK, cols), 1)
+    here = jnp.where(lane % TOK == t, 1.0, 0.0)
+
+    def along(values):
+        return jnp.dot(values, here, precision=lax.Precision.HIGHEST, preferred_element_type=F32)
+
+    ids_along = along(ids_ref[...].astype(F32)) + 1.0
+    own_ids = [ids_along[k : k + 1] for k in range(2)]
+    masked = [jnp.where(iota((1, cols), 1) // BLOCK == z, v, 0.0) for v in own_ids]
+    lines = [v[:, 128 * k : 128 * k + 128] for v in masked for k in range(3)]
+    meta[xl, z] = jnp.concatenate(lines + [jnp.zeros((2, 128), F32)], axis=0)
     hpad = dense_w.shape[2]
     zero = jnp.zeros((hpad - hid, feat), F32)
     for k, ref in enumerate((dg_ref, du_ref, dd_ref)):
@@ -109,109 +119,116 @@
     def zpos(p):
         return at_z(-p) if p <= 4 else at_z(p - 4)
 
+    def token_send(x, p, sems, to):
+        send, recv = sems
+        zs = zpos(p)
+        start(toks.at[x, zs], toks.at[x, zs], send.at[0], recv.at[0], to)
+        start(meta.at[x, zs], meta.at[x, zs], send.at[1], recv.at[1], to)
+
+    def token_wait(x, p, recv):
+        zs = zpos(p)
+        arrived(toks.at[x, zs], recv.at[0])
+        arrived(meta.at[x, zs], recv.at[1])
+
+    def token_sems(d, step):
+        i = (1 - d) // 2
+        return s1.at[i, step - 1], r1.at[i, step - 1]
+
     def token_hop(d, step):
-        zs = at_z(-d * (step - 1))
-        i = (1 - d) // 2
-        start(toks.at[xl, zs], toks.at[xl, zs], s1.at[i, step - 1, 0], r1.at[i, step - 1, 0], ring(d))
-        start(meta.at[xl, zs], meta.at[xl, zs], s1.at[i, step - 1, 1], r1.at[i, step - 1, 1], ring(d))
-
-    def token_wait(d, step):
-        zs = at_z(-d * step)
-        i = (1 - d) // 2
-        arrived(toks.at[xl, zs], r1.at[i, step - 1, 0])
-        arrived(meta.at[xl, zs], r1.at[i, step - 1, 1])
+        p = 0 if step == 1 else (step - 1 if d == 1 else step + 3)
+        token_send(xl, p, token_sems(d, step), ring(d))
+
+    def token_arrival(d, step):
+        token_wait(xl, step if d == 1 else step + 4, token_sems(d, step)[1])
 
     def token_x(p):
-        zs = zpos(p)
-        start(toks.at[xl, zs], toks.at[xl, zs], x_s.at[p, 0], x_r.at[p, 0], x_dev)
-        start(meta.at[xl, zs], meta.at[xl, zs], x_s.at[p, 1], x_r.at[p, 1], x_dev)
-
+        token_send(xl, p, (x_s.at[p], x_r.at[p]), x_dev)
+
+    token_x(0)
     token_hop(1, 1)
     token_hop(-1, 1)
-    token_x(0)
     for k in range(3):
         start(dense_w.at[k, c], dense_w.at[k, c], dw_s.at[k], dw_r.at[k], core_dev)
     for step in range(1, 5):
-        token_wait(1, step)
-        if step < 4:
-            token_hop(1, step + 1)
-        token_x(step)
-        if step < 4:
-            token_wait(-1, step)
-            if step < 3:
-                token_hop(-1, step + 1)
-            token_x(step + 4)
-    for p in range(NZ):
-        zs = zpos(p)
-        arrived(toks.at[1 - xl, zs], x_r.at[p, 0])
-        arrived(meta.at[1 - xl, zs], x_r.at[p, 1])
+        for d in (1, -1):
+            if step == 4 and d == -1:
+                continue
+            token_arrival(d, step)
+            if step < 3 or step == 3 and d == 1:
+                token_hop(d, step + 1)
+            token_x(step if d == 1 else step + 4)
 
     y, xh = h // 2, h % 2
+    par = z % 2
 
     def plane(dy, flip):
         return lax.rem(y + dy + 8, 4) * 2 + (1 - xh if flip else xh)
 
-    targets = (plane(-z, True), plane(2, False), plane(1, False), plane(-1, False), h)
-    cols = NZ * BLOCK
+    def column(o):
+        return 1 - xl if o else xl
+
+    targets = ((plane(-z, True), 0), (plane(-z, True), 1), (plane(1, False), 1 - par), (plane(-1, False), par), (plane(2, False), par))
     row = iota((8, cols), 0)
     label = jnp.full((8, cols), -1, jnp.int32)
-    for i, q in enumerate(targets):
+    for i, (q, _) in enumerate(targets + ((h, 0),)):
         label = jnp.where(row == i, q + 1, label)
     label = label.astype(F32)
     a, b = iota((cols, cols), 0), iota((cols, cols), 1)
     before = jnp.where(a // TOK == b // TOK, jnp.where(a < b, 1.0, 0.0), 0.0).astype(BF)
-    matches, ranks = [], []
-    for x in range(2):
+    r, t = iota((PIECE, cols), 0), iota((PIECE, cols), 1)
+    slot = (r % CAP).astype(F32)
+    group, base = t // TOK, r // CAP * 2
+
+    slices = (
+        h, plane(2, False), plane(-1, False), plane(1, False),
+        plane(z, True), plane(z - 1, True), plane(z + 1, True), plane(z + 2, True),
+    )
+
+    def tensor(p, j):
+        if p in (1, 3):
+            return 1 - par if j else par
+        if p == 2:
+            return par if j else 1 - par
+        return j
+
+    def chunk(p, k):
+        return rows.at[slices[p], c, tensor(p, k // 2), column(k % 2)]
+
+    def core_send(p, k):
+        start(chunk(p, k), chunk(p, k), core_s.at[p, k], core_r.at[p, k], core_dev)
+
+    def hop(d, p, k, i):
+        j = (1 - d) // 2
+        start(chunk(p, k), chunk(p, k), ring_s.at[j, i], ring_r.at[j, i], ring(d))
+
+    for o in range(2):
+        x = column(o)
+        if o:
+            for p in (0, 1, 5, 2, 6, 3, 7, 4):
+                token_wait(x, p, x_r.at[p])
         info = meta[x, 0]
         for k in range(1, NZ):
             info = info + meta[x, k]
-        match = jnp.where(info[0:1] == label, 1.0, jnp.where(info[1:2] == label, 1.0, 0.0))
-        matches.append(match)
-        ranks.append(jnp.dot(match.astype(BF), before, preferred_element_type=F32))
-    r, t = iota((2 * PIECE, cols), 0), iota((2 * PIECE, cols), 1)
-    slot = (r % CAP).astype(F32)
-    inside = t // TOK == (r % PIECE) // CAP * 2 + r // PIECE
-
-    def chosen(i, x):
-        choose = jnp.where(inside, jnp.where(ranks[x][i : i + 1] == slot, matches[x][i : i + 1], 0.0), 0.0)
+        ids = [jnp.concatenate([info[i : i + 1] for i in range(3 * k, 3 * k + 3)], axis=1) for k in range(2)]
+        match = jnp.where(ids[0] == label, 1.0, jnp.where(ids[1] == label, 1.0, 0.0))
+        rank = jnp.dot(match.astype(BF), before, preferred_element_type=F32)
         every = toks[x].reshape(cols, feat)
-        both = jnp.dot(choose.astype(BF), every, preferred_element_type=F32).astype(BF)
-        return both.reshape(2, PIECE, feat)
-
-    for i in range(4):
-        for x in range(2):
-            both = chosen(i, x)
-            for k in range(2):
-                pick[i, k, x] = both[k]
+
+        def chosen(i, which):
+            choose = jnp.where(rank[i : i + 1] == slot, match[i : i + 1], 0.0)
+            choose = jnp.where(group == base + which, choose, 0.0).astype(BF)
+            return jnp.dot(choose, every, preferred_element_type=F32).astype(BF)
+
+        for i, (q, which) in enumerate(targets):
+            pick[i, o] = chosen(i, which)
+            start(pick.at[i, o], rows.at[h, c, which, x], s3.at[i, o], r3.at[i, o], (e, q))
+        for k in range(2):
+            rows[h, c, k, x] = chosen(len(targets), k)
+            core_send(0, 2 * k + o)
+
+    def accumulate(p, first=False):
         for k in range(4):
-            start(
-                pick.at[i, k // 2, k % 2], rows.at[h, c, k // 2, k % 2], s3.at[i, k], r3.at[i, k],
-                (e, targets[i]),
-            )
-    for x in range(2):
-        both = chosen(4, x)
-        for k in range(2):
-            rows[h, c, k, x] = both[k]
-
-    slices = (h, plane(-2, False), plane(-1, False), plane(1, False), plane(z, True), plane(z - 1, True), plane(z + 1, True), plane(z + 2, True))
-
-    def chunk(p, k):
-        return rows.at[slices[p], c, k // 2, k % 2]
-
-    def core_send(p, k):
-        start(chunk(p, k), chunk(p, k), core_s.at[p, k], core_r.at[p, k], core_dev)
-
-    def hop(d, step, k):
-        ref = chunk(4 if step == 0 else (5 if d == 1 else 6), k)
-        i = (1 - d) // 2
-        start(ref, ref, ring_s.at[i, step, k], ring_r.at[i, step, k], ring(d))
-
-    def multiply(p):
-        for k in range(4):
-            arrived(rows.at[slices[p], 1 - c, k // 2, k % 2], core_r.at[p, k])
-
-    def accumulate(p, first=False):
-        multiply(p)
+            arrived(rows.at[slices[p], 1 - c, tensor(p, k // 2), column(k % 2)], core_r.at[p, k])
         sl = slices[p]
         col = pl.ds(pl.multiple_of(sl * feat, 128), feat)
         x = rows[sl, :, 0].reshape(4 * PIECE, feat)
@@ -220,66 +237,75 @@
             new = lax.dot_general(lhs, w[:, col], NT, preferred_element_type=F32)
             pre[k] = new if first else pre[k] + new
 
-    for k in range(4):
-        core_send(0, k)
-
-    for k in range(3):
-        arrived(dense_w.at[k, 1 - c], dw_r.at[k])
-    every = toks[...].reshape(2 * cols, feat)
-    for k in range(3):
-        w = dense_w[k].reshape(2 * hpad, feat)
-        part = lax.dot_general(every, w, NT, preferred_element_type=F32).reshape(2, NZ, BLOCK, 2 * hpad)
-        part = part[:, :, 0:TOK] if k < 2 else part[:, :, TOK:BLOCK]
-        for hh in range(NH):
-            part_out[hh, k] = jnp.concatenate([part[0, hh], part[1, hh]], 0).astype(BF)
-    for k in range(1, NH):
-        hh = lax.rem(h + k, NH)
-        start(part_out.at[hh], part_in.at[k], da_s.at[k], da_r.at[k], (e, hh))
-
-    for k in range(4):
-        arrived(chunk(4, k), r3.at[0, k])
-        hop(1, 0, k)
-        hop(-1, 0, k)
-        core_send(4, k)
-
+    def dense_part():
+        for k in range(3):
+            arrived(dense_w.at[k, 1 - c], dw_r.at[k])
+        every = toks[...].reshape(2 * cols, feat)
+        for k in range(3):
+            w = dense_w[k].reshape(2 * hpad, feat)
+            part = lax.dot_general(every, w, NT, preferred_element_type=F32).reshape(2, NZ, BLOCK, 2 * hpad)
+            part = part[:, :, 0:TOK] if k < 2 else part[:, :, TOK:BLOCK]
+            for hh in range(NH):
+                part_out[hh, k] = jnp.concatenate([part[0, hh], part[1, hh]], 0).astype(BF)
+        for k in range(1, NH):
+            hh = lax.rem(h + k, NH)
+            start(part_out.at[hh], part_in.at[k], da_s.at[k], da_r.at[k], (e, hh))
+
+    for o in range(2):
+        for k in range(2):
+            arrived(chunk(4, 2 * k + o), r3.at[k, o])
+            hop(1, 4, 2 * k + o, 2 * k + o)
+            hop(-1, 4, 2 * k + o, 2 * k + o)
+            core_send(4, 2 * k + o)
+        for m, p, d in ((2, 2, -1), (3, 3, 1)):
+            arrived(chunk(p, o), r3.at[m, o])
+            hop(d, p, o, 6 + o)
+            core_send(p, o)
+        arrived(chunk(1, o), r3.at[4, o])
+        hop(-1 if o else 1, 1, o, 8)
+        core_send(1, o)
+
+    dense_part()
     for load in loads:
         load.wait()
-    accumulate(0, True)
-
-    for i in (2, 3):
-        for k in range(4):
-            arrived(chunk(i, k), r3.at[i, k])
-            core_send(i, k)
-    for k in range(4):
-        for d in (1, -1):
-            arrived(chunk(5 if d == 1 else 6, k), ring_r.at[(1 - d) // 2, 0, k])
-            if (k < 2) == (d == 1):
-                hop(d, 1, k)
-            core_send(5 if d == 1 else 6, k)
+    for o in range(2):
+        for k in range(2):
+            for d in (1, -1):
+                p = 5 if d == 1 else 6
+                arrived(chunk(p, 2 * k + o), ring_r.at[(1 - d) // 2, 2 * k + o])
+                if (k == 0) == (d == 1):
+                    hop(d, p, 2 * k + o, 4 + o)
+                core_send(p, 2 * k + o)
+        if o == 0:
+            accumulate(0, True)
+    for o in range(2):
+        for p, d in ((2, 1), (3, -1)):
+            other = 5 - p
+            arrived(chunk(other, 2 + o), ring_r.at[(1 - d) // 2, 6 + o])
+            core_send(other, 2 + o)
+        arrived(chunk(1, 2 + o), ring_r.at[o, 8])
+        core_send(1, 2 + o)
     accumulate(4)
-    accumulate(2)
-    accumulate(3)
-    for k in range(4):
-        arrived(chunk(1, k), r3.at[1, k])
-        core_send(1, k)
-    for k in range(4):
-        arrived(chunk(7, k), ring_r.at[k // 2, 1, k])
-        core_send(7, k)
     accumulate(5)
     accumulate(6)
+    for k in range(2):
+        for o in range(2):
+            arrived(chunk(7, 2 * k + o), ring_r.at[k, 4 + o])
+            core_send(7, 2 * k + o)
+        accumulate(3 - k)
     accumulate(1)
-
-    sums = part_out[h].astype(F32)
-    for k in range(1, NH):
-        arrived(part_in.at[k], da_r.at[k])
-        sums = sums + part_in[k].astype(F32)
-    dense_gate, dense_up = grads_of(sums[0], sums[1], sums[2])
-    dgrad[0, h] = dense_gate
-    dgrad[1, h] = dense_up
-    for k in range(1, NH):
-        start(dgrad.at[:, h], dgrad.at[:, h], db_s.at[k], db_r.at[k], (e, lax.rem(h + k, NH)))
-
     accumulate(7)
+
+    def dense_sum():
+        sums = part_out[h].astype(F32)
+        for k in range(1, NH):
+            arrived(part_in.at[k], da_r.at[k])
+            sums = sums + part_in[k].astype(F32)
+        dense_gate, dense_up = grads_of(sums[0], sums[1], sums[2])
+        dgrad[0, h] = dense_gate
+        dgrad[1, h] = dense_up
+        for k in range(1, NH):
+            start(dgrad.at[:, h], dgrad.at[:, h], db_s.at[k], db_r.at[k], (e, lax.rem(h + k, NH)))
 
     def dense_result():
         for k in range(1, NH):
@@ -344,6 +370,7 @@
     def exchanged(i):
         arrived(got.at[i], ex_r.at[i])
 
+    dense_sum()
     produce(0)
     produce(1)
     exchanged(0)
@@ -369,8 +396,6 @@
             produce(i + 3)
         if step == 2:
             dense_result()
-        if step == 3:
-            dense_reduce()
     exchanged(7)
     for x in range(2):
         value = mine(7, x)
@@ -380,6 +405,7 @@
         total[x] = value
     x_out[...] = total[1 - xl].astype(BF)
     start(x_out, x_in, xx_s.at[0], xx_r.at[0], x_dev)
+    dense_reduce()
     r, t = iota((NZ * 16, PIECE), 0), iota((NZ * 16, PIECE), 1)
     spread = jnp.where(r % 16 < CAP, jnp.where(t == (r // 16) * CAP + r % 16, 1.0, 0.0), 0.0).astype(BF)
     arrived(x_in, xx_r.at[0])
@@ -402,8 +428,9 @@
         stay.start()
 
     n = NZ * 16
-    ids0, ids1 = meta_ref[0:1, 0:n], meta_ref[1:2, 0:n]
-    g0, g1 = meta_ref[2:3, 0:n], meta_ref[3:4, 0:n]
+    ids0, ids1 = own_ids[0][:, 0:n], own_ids[1][:, 0:n]
+    gates = along(gates_ref[...])
+    g0, g1 = gates[0:1, 0:n], gates[1:2, 0:n]
     r, t = iota((n, n), 0), iota((n, n), 1)
     label = ((h + (z - r // 16 + NZ) % NZ) % NH + 1).astype(F32)
     hit0, hit1 = jnp.where(ids0 == label, 1.0, 0.0), jnp.where(ids1 == label, 1.0, 0.0)
@@ -441,14 +468,12 @@
     feat = tokens.shape[1]
     hid, width = expert_gate.shape[1], expert_gate.shape[2]
     hpad = (hid + 15) // 16 * 16
-    meta = jnp.concatenate([route_ids.astype(F32) + 1.0, route_gates], axis=1).T
-    meta = jnp.tile(jnp.pad(meta, ((0, 4), (0, 0))), (1, 2 * NZ))
     dma, vmem = pltpu.SemaphoreType.DMA, pltpu.VMEM
     scratch = [
         vmem((hid, width), BF), vmem((hid, width), BF), vmem((hid, width), BF),
         vmem((2, NZ, BLOCK, feat), BF),
-        vmem((2, NZ, 8, NZ * BLOCK), F32),
-        vmem((4, 2, 2, PIECE, feat), BF),
+        vmem((2, NZ, 8, 128), F32),
+        vmem((5, 2, PIECE, feat), BF),
         vmem((NH, 2, 2, 2, PIECE, feat), BF),
         vmem((3, 4 * PIECE, hid), F32),
         vmem((4 * PIECE, hid), BF), vmem((4 * PIECE, hid), BF),
@@ -464,8 +489,8 @@
         vmem((2, NZ, TOK, feat), F32),
         vmem((NZ * TOK, feat), BF), vmem((NZ * TOK, feat), BF),
         vmem((NZ, PAD, feat), BF), vmem((NZ, PAD, feat), BF),
-        dma((3,)), dma((2, 4, 2)), dma((2, 4, 2)), dma((4, 4)), dma((4, 4)),
-        dma((2, 2, 4)), dma((2, 2, 4)), dma((8, 2)), dma((8, 2)), dma((8, 4)), dma((8, 4)),
+        dma((3,)), dma((2, 4, 2)), dma((2, 4, 2)), dma((5, 2)), dma((5, 2)),
+        dma((2, 9)), dma((2, 9)), dma((8, 2)), dma((8, 2)), dma((8, 4)), dma((8, 4)),
         dma((3,)), dma((3,)), dma((8,)), dma((8,)), dma((8,)), dma((8,)), dma((8,)), dma((8,)),
         dma((8,)), dma((8,)), dma((2, 4, 2)), dma((2, 4, 2)), dma((2,)), dma((2,)), dma((9,)), dma((9,)),
     ]
@@ -473,12 +498,12 @@
     return pl.pallas_call(
         kernel,
         out_shape=jax.ShapeDtypeStruct(tokens.shape, BF),
-        in_specs=[whole] * 3 + [far] * 3 + [whole] * 3,
+        in_specs=[whole] * 4 + [far] * 3 + [whole] * 3,
         out_specs=whole,
         scratch_shapes=scratch,
         compiler_params=pltpu.CompilerParams(collective_id=0, has_side_effects=True, vmem_limit_bytes=56 << 20),
         name="layer",
-    )(tokens, cotangent, meta, expert_gate, expert_up, expert_down, dense_gate, dense_up, dense_down)
+    )(tokens, cotangent, route_ids.T, route_gates.T, expert_gate, expert_up, expert_down, dense_gate, dense_up, dense_down)
 
 
 def solution(mesh):

time: 140 us -> 122 us (0.87); the launches traced: 138 us -> 122 us
  Pallas kernels: 134 us -> 121 us
    pallas_call x1, Pallas kernels: 134 us -> 121 us  [on_device(): pl.pallas_call(kernel, out_shape=jax.ShapeDtypeStruct(tokens.shape, BF),...]
where the time goes in v3:
time: 122 us
  Pallas kernels  121 us (99%)
  local copies, waits for them, and re-layouts  1.41 us (1%)
    pallas_call x1, Pallas kernels, on_device(): pl.pallas_call(kernel, out_shape=jax.ShapeDtypeStruct(tokens.shape, BF),...  121 us

profile of v3, /device:TPU:6, one launch (start us, length us, event | category | flops | bytes accessed | tf_op | source)
XLA Modules:
  0.0 121.9 jit_solution(6068363553984360071)
XLA Ops:
  0.0 120.5 %layer.1 = bf16[24,896]{1,0:T(8,128)(2,1)} custom-call(bf16[24,896]{1,0:T(8,128)(2,1)} %tok_ref.1, bf16[24,896]{1,0:T(8,128)(2,1)} %cot_ref.1, s32[2,24]{1,0:T(2,128)} %bitcast.2, f32[2,24]{1,0:T(2,128)} %bitcast.3, bf16[1,152,7168]{2,1,0:T(8,128)(2,1)} %wg_hbm.1, bf16[1,152,7168]{2,1,0:T(8,128)(2,1)} %wu_hbm.1, bf16[1,152,7168]{2,1,0:T(8,128)(2,1)} %wd_hbm.1, ...), custom_call_target="tpu_custom_call" | custom-call | tf_op jit(solution)/shard_map/layer/pallas_call | solution.py:498
  120.5 1.4 %copy.12 = bf16[24,896]{1,0:T(8,128)(2,1)} copy(bf16[24,896]{1,0:T(8,128)(2,1)} %layer.1) | data formatting | bytes 86016

commit v4 on v3

--- a/solution.py
+++ b/solution.py
@@ -30,10 +30,10 @@
 
 def kernel(
     tok_ref, cot_ref, ids_ref, gates_ref, wg_hbm, wu_hbm, wd_hbm, dg_ref, du_ref, dd_ref, out_ref,
-    wg, wu, wd, toks, meta, pick, rows, pre, gg, gu, keep, give, got, chain_out, chain_in, total,
+    wg, wu, wd, toks, meta, pick, rows, pre, gg, gu, keep, give, got, chain_out, chain_in, side_out, side_in, rest_out, rest_in, total,
     x_out, x_in, home_out, home_in, dense_w, part_out, part_in, dgrad, res, res_x_out, res_x_in, res_out, res_in,
     w_sem, s1, r1, s3, r3, ring_s, ring_r, x_s, x_r, core_s, core_r, dw_s, dw_r, da_s, da_r, db_s, db_r, dz_s, dz_r,
-    ex_s, ex_r, ch_s, ch_r, xx_s, xx_r, hm_s, hm_r,
+    ex_s, ex_r, ch_s, ch_r, sd_s, sd_r, rs_s, rs_r, xx_s, xx_r, hm_s, hm_r,
 ):
     e, h = lax.axis_index("expert"), lax.axis_index("hidden")
     z, xl, c = e // 4, (e // 2) % 2, e % 2
@@ -119,43 +119,44 @@
     def zpos(p):
         return at_z(-p) if p <= 4 else at_z(p - 4)
 
+    def token_parts(x, p):
+        zs = zpos(p)
+        return [meta.at[x, zs]] + [toks.at[x, zs, pl.ds(16 * k, 16)] for k in range(BLOCK // 16)]
+
     def token_send(x, p, sems, to):
-        send, recv = sems
-        zs = zpos(p)
-        start(toks.at[x, zs], toks.at[x, zs], send.at[0], recv.at[0], to)
-        start(meta.at[x, zs], meta.at[x, zs], send.at[1], recv.at[1], to)
+        for k, ref in enumerate(token_parts(x, p)):
+            start(ref, ref, sems[0].at[k], sems[1].at[k], to)
 
     def token_wait(x, p, recv):
-        zs = zpos(p)
-        arrived(toks.at[x, zs], recv.at[0])
-        arrived(meta.at[x, zs], recv.at[1])
+        for k, ref in enumerate(token_parts(x, p)):
+            arrived(ref, recv.at[k])
 
     def token_sems(d, step):
         i = (1 - d) // 2
         return s1.at[i, step - 1], r1.at[i, step - 1]
 
-    def token_hop(d, step):
-        p = 0 if step == 1 else (step - 1 if d == 1 else step + 3)
-        token_send(xl, p, token_sems(d, step), ring(d))
-
-    def token_arrival(d, step):
-        token_wait(xl, step if d == 1 else step + 4, token_sems(d, step)[1])
+    def token_pass(d, step):
+        p = step + 4 if d == -1 and step else step
+        for k, ref in enumerate(token_parts(xl, p)):
+            if step:
+                arrived(ref, token_sems(d, step)[1].at[k])
+            if step < (4 if d == 1 else 3):
+                send, recv = token_sems(d, step + 1)
+                start(ref, ref, send.at[k], recv.at[k], ring(d))
 
     def token_x(p):
         token_send(xl, p, (x_s.at[p], x_r.at[p]), x_dev)
 
+    token_pass(1, 0)
+    token_pass(-1, 0)
     token_x(0)
-    token_hop(1, 1)
-    token_hop(-1, 1)
     for k in range(3):
         start(dense_w.at[k, c], dense_w.at[k, c], dw_s.at[k], dw_r.at[k], core_dev)
     for step in range(1, 5):
         for d in (1, -1):
             if step == 4 and d == -1:
                 continue
-            token_arrival(d, step)
-            if step < 3 or step == 3 and d == 1:
-                token_hop(d, step + 1)
+            token_pass(d, step)
             token_x(step if d == 1 else step + 4)
 
     y, xh = h // 2, h % 2
@@ -304,12 +305,20 @@
         dense_gate, dense_up = grads_of(sums[0], sums[1], sums[2])
         dgrad[0, h] = dense_gate
         dgrad[1, h] = dense_up
-        for k in range(1, NH):
-            start(dgrad.at[:, h], dgrad.at[:, h], db_s.at[k], db_r.at[k], (e, lax.rem(h + k, NH)))
+        start(dgrad.at[:, h], dgrad.at[:, h], db_s.at[0], db_r.at[0], (e, plane(0, True)))
+        for k in range(1, 4):
+            start(dgrad.at[:, h], dgrad.at[:, h], db_s.at[k], db_r.at[k], (e, plane(k, False)))
+
+    def dense_pass():
+        ref = dgrad.at[:, plane(0, True)]
+        arrived(ref, db_r.at[0])
+        for k in range(1, 4):
+            start(ref, ref, db_s.at[3 + k], db_r.at[3 + k], (e, plane(k, False)))
 
     def dense_result():
-        for k in range(1, NH):
-            arrived(dgrad.at[:, lax.rem(h + NH - k, NH)], db_r.at[k])
+        for k in range(1, 4):
+            arrived(dgrad.at[:, plane(-k, False)], db_r.at[k])
+            arrived(dgrad.at[:, plane(-k, True)], db_r.at[3 + k])
         result = None
         for k in range(2):
             lhs = dgrad[k].reshape(cols, 2 * hpad)
@@ -355,35 +364,51 @@
         start(give.at[i], got.at[i], ex_s.at[i], ex_r.at[i], core_dev)
         keep[i] = rows_of(c).reshape(2, PIECE, feat)
 
-    def mine(i, x):
-        return keep[i, x] + got[i, x].astype(F32)
+    cut = chain_out.shape[4]
+
+    def settle(i):
+        arrived(got.at[i], ex_r.at[i])
+        keep[i] = keep[i] + got[i].astype(F32)
+        side_out[i] = keep[i, 1 - xl, :, cut:feat].astype(BF)
+        start(side_out.at[i], side_in.at[i], sd_s.at[i], sd_r.at[i], x_dev)
 
     def chain(d, step, x, i):
         k = (1 - d) // 2
-        value = mine(i, x)
+        value = keep[i, x, :, 0:cut]
         if step == 1 and x == k or step > 1:
             arrived(chain_in.at[k, step - 1, x], ch_r.at[k, step - 1, x])
             value = value + chain_in[k, step - 1, x].astype(F32)
         chain_out[k, step, x] = value.astype(BF)
         start(chain_out.at[k, step, x], chain_in.at[k, step, x], ch_s.at[k, step, x], ch_r.at[k, step, x], ring(d))
 
-    def exchanged(i):
-        arrived(got.at[i], ex_r.at[i])
+    def side(i):
+        arrived(side_in.at[i], sd_r.at[i])
+        return keep[i, xl, :, cut:feat] + side_in[i].astype(F32)
+
+    def side_chain(d, step, i):
+        k = (1 - d) // 2
+        value = side(i)
+        if step > k:
+            arrived(rest_in.at[k, step - 1], rs_r.at[k, step - 1])
+            value = value + rest_in[k, step - 1].astype(F32)
+        rest_out[k, step] = value.astype(BF)
+        start(rest_out.at[k, step], rest_in.at[k, step], rs_s.at[k, step], rs_r.at[k, step], ring(d))
 
     dense_sum()
     produce(0)
     produce(1)
-    exchanged(0)
+    settle(0)
     chain(1, 0, 0, 0)
     chain(-1, 0, 1, 0)
     produce(2)
+    dense_pass()
     for step in range(1, 4):
         i = 2 * step - 1
-        exchanged(i)
+        settle(i)
         if step == 1:
             chain(1, 1, 1, i)
         produce(i + 2)
-        exchanged(i + 1)
+        settle(i + 1)
         if step == 1:
             chain(-1, 1, 0, i + 1)
             chain(1, 1, 0, i)
@@ -394,23 +419,34 @@
                 chain(-1, step, 1 - x, i + 1)
         if i + 3 < 8:
             produce(i + 3)
+        if step > 1:
+            side_chain(-1, step - 1, i - 1)
+        side_chain(1, step - 1, max(i - 2, 0))
         if step == 2:
             dense_result()
-    exchanged(7)
+        if step == 3:
+            dense_reduce()
+    settle(7)
     for x in range(2):
-        value = mine(7, x)
+        value = keep[7, x, :, 0:cut]
         for k in range(2):
             arrived(chain_in.at[k, 3, x], ch_r.at[k, 3, x])
             value = value + chain_in[k, 3, x].astype(F32)
         total[x] = value
     x_out[...] = total[1 - xl].astype(BF)
     start(x_out, x_in, xx_s.at[0], xx_r.at[0], x_dev)
-    dense_reduce()
+    side_chain(-1, 3, 6)
+    side_chain(1, 3, 5)
+    rest = side(7)
+    for k in range(2):
+        arrived(rest_in.at[k, 3], rs_r.at[k, 3])
+        rest = rest + rest_in[k, 3].astype(F32)
     r, t = iota((NZ * 16, PIECE), 0), iota((NZ * 16, PIECE), 1)
     spread = jnp.where(r % 16 < CAP, jnp.where(t == (r // 16) * CAP + r % 16, 1.0, 0.0), 0.0).astype(BF)
     arrived(x_in, xx_r.at[0])
-    final = (total[xl] + x_in[...].astype(F32)).astype(BF)
-    home_out[...] = jnp.dot(spread, final, preferred_element_type=F32).astype(BF).reshape(NZ, 16, feat)
+    first = total[xl] + x_in[...].astype(F32)
+    for lo, hi, value in ((0, cut, first), (cut, feat, rest)):
+        home_out[:, :, lo:hi] = jnp.dot(spread, value.astype(BF), preferred_element_type=F32).astype(BF).reshape(NZ, 16, hi - lo)
 
     back = lax.rem(h - z + NH, NH)
     for k in range(1, NZ):
@@ -468,6 +504,7 @@
     feat = tokens.shape[1]
     hid, width = expert_gate.shape[1], expert_gate.shape[2]
     hpad = (hid + 15) // 16 * 16
+    cut = feat // 128 * 4 // 7 * 128
     dma, vmem = pltpu.SemaphoreType.DMA, pltpu.VMEM
     scratch = [
         vmem((hid, width), BF), vmem((hid, width), BF), vmem((hid, width), BF),
@@ -479,9 +516,11 @@
         vmem((4 * PIECE, hid), BF), vmem((4 * PIECE, hid), BF),
         vmem((NZ, 2, PIECE, feat), F32),
         vmem((NZ, 2, PIECE, feat), BF), vmem((NZ, 2, PIECE, feat), BF),
-        vmem((2, 4, 2, PIECE, feat), BF), vmem((2, 4, 2, PIECE, feat), BF),
-        vmem((2, PIECE, feat), F32),
-        vmem((PIECE, feat), BF), vmem((PIECE, feat), BF),
+        vmem((2, 4, 2, PIECE, cut), BF), vmem((2, 4, 2, PIECE, cut), BF),
+        vmem((NZ, PIECE, feat - cut), BF), vmem((NZ, PIECE, feat - cut), BF),
+        vmem((2, 4, PIECE, feat - cut), BF), vmem((2, 4, PIECE, feat - cut), BF),
+        vmem((2, PIECE, cut), F32),
+        vmem((PIECE, cut), BF), vmem((PIECE, cut), BF),
         vmem((NZ, 16, feat), BF), vmem((NZ, 16, feat), BF),
         vmem((3, 2, hpad, feat), BF),
         vmem((NH, 3, BLOCK, 2 * hpad), BF), vmem((NH, 3, BLOCK, 2 * hpad), BF),
@@ -489,10 +528,11 @@
         vmem((2, NZ, TOK, feat), F32),
         vmem((NZ * TOK, feat), BF), vmem((NZ * TOK, feat), BF),
         vmem((NZ, PAD, feat), BF), vmem((NZ, PAD, feat), BF),
-        dma((3,)), dma((2, 4, 2)), dma((2, 4, 2)), dma((5, 2)), dma((5, 2)),
-        dma((2, 9)), dma((2, 9)), dma((8, 2)), dma((8, 2)), dma((8, 4)), dma((8, 4)),
+        dma((3,)), dma((2, 4, 4)), dma((2, 4, 4)), dma((5, 2)), dma((5, 2)),
+        dma((2, 9)), dma((2, 9)), dma((8, 4)), dma((8, 4)), dma((8, 4)), dma((8, 4)),
         dma((3,)), dma((3,)), dma((8,)), dma((8,)), dma((8,)), dma((8,)), dma((8,)), dma((8,)),
-        dma((8,)), dma((8,)), dma((2, 4, 2)), dma((2, 4, 2)), dma((2,)), dma((2,)), dma((9,)), dma((9,)),
+        dma((8,)), dma((8,)), dma((2, 4, 2)), dma((2, 4, 2)), dma((8,)), dma((8,)), dma((2, 4)), dma((2, 4)),
+        dma((2,)), dma((2,)), dma((9,)), dma((9,)),
     ]
     whole, far = pl.BlockSpec(memory_space=pltpu.VMEM), pl.BlockSpec(memory_space=pl.ANY)
     return pl.pallas_call(

time: 122 us -> 118 us (0.967); the launches traced: 122 us -> 116 us
  Pallas kernels: 121 us -> 114 us
    pallas_call x1, Pallas kernels: 121 us -> 114 us  [on_device(): pl.pallas_call(kernel, out_shape=jax.ShapeDtypeStruct(tokens.shape, BF),...]
where the time goes in v4:
time: 118 us; the launch traced here: 116 us
  Pallas kernels  114 us (97%)
  local copies, waits for them, and re-layouts  1.41 us (1%)
    pallas_call x1, Pallas kernels, on_device(): pl.pallas_call(kernel, out_shape=jax.ShapeDtypeStruct(tokens.shape, BF),...  114 us

profile of v4, /device:TPU:6, one launch (start us, length us, event | category | flops | bytes accessed | tf_op | source)
XLA Modules:
  0.0 115.6 jit_solution(373057149977773603)
XLA Ops:
  0.0 114.2 %layer.1 = bf16[24,896]{1,0:T(8,128)(2,1)} custom-call(bf16[24,896]{1,0:T(8,128)(2,1)} %tok_ref.1, bf16[24,896]{1,0:T(8,128)(2,1)} %cot_ref.1, s32[2,24]{1,0:T(2,128)} %bitcast.2, f32[2,24]{1,0:T(2,128)} %bitcast.3, bf16[1,152,7168]{2,1,0:T(8,128)(2,1)} %wg_hbm.1, bf16[1,152,7168]{2,1,0:T(8,128)(2,1)} %wu_hbm.1, bf16[1,152,7168]{2,1,0:T(8,128)(2,1)} %wd_hbm.1, ...), custom_call_target="tpu_custom_call" | custom-call | tf_op jit(solution)/shard_map/layer/pallas_call | solution.py:538
  114.2 1.4 %copy.12 = bf16[24,896]{1,0:T(8,128)(2,1)} copy(bf16[24,896]{1,0:T(8,128)(2,1)} %layer.1) | data formatting | bytes 86016

commit v5 on v4

--- a/solution.py
+++ b/solution.py
@@ -504,7 +504,7 @@
     feat = tokens.shape[1]
     hid, width = expert_gate.shape[1], expert_gate.shape[2]
     hpad = (hid + 15) // 16 * 16
-    cut = feat // 128 * 4 // 7 * 128
+    cut = feat // 128 * 3 // 7 * 128
     dma, vmem = pltpu.SemaphoreType.DMA, pltpu.VMEM
     scratch = [
         vmem((hid, width), BF), vmem((hid, width), BF), vmem((hid, width), BF),

time: 118 us -> 117 us (level)
  no operation moved by 1% of the time
where the time goes in v5:
time: 117 us; the launch traced here: 116 us
  Pallas kernels  114 us (97%)
  local copies, waits for them, and re-layouts  1.41 us (1%)
    pallas_call x1, Pallas kernels, on_device(): pl.pallas_call(kernel, out_shape=jax.ShapeDtypeStruct(tokens.shape, BF),...  114 us

profile of v5, /device:TPU:6, one launch (start us, length us, event | category | flops | bytes accessed | tf_op | source)
XLA Modules:
  0.0 115.5 jit_solution(9818289127559980853)
XLA Ops:
  0.0 114.1 %layer.1 = bf16[24,896]{1,0:T(8,128)(2,1)} custom-call(bf16[24,896]{1,0:T(8,128)(2,1)} %tok_ref.1, bf16[24,896]{1,0:T(8,128)(2,1)} %cot_ref.1, s32[2,24]{1,0:T(2,128)} %bitcast.2, f32[2,24]{1,0:T(2,128)} %bitcast.3, bf16[1,152,7168]{2,1,0:T(8,128)(2,1)} %wg_hbm.1, bf16[1,152,7168]{2,1,0:T(8,128)(2,1)} %wu_hbm.1, bf16[1,152,7168]{2,1,0:T(8,128)(2,1)} %wd_hbm.1, ...), custom_call_target="tpu_custom_call" | custom-call | tf_op jit(solution)/shard_map/layer/pallas_call | solution.py:538
  114.1 1.4 %copy.12 = bf16[24,896]{1,0:T(8,128)(2,1)} copy(bf16[24,896]{1,0:T(8,128)(2,1)} %layer.1) | data formatting | bytes 86016
